TPU v7x, 128 devices: a whole 4x4x4 slice. The times are simulated.
128 devices in a mesh: pp: 16 (over y_hi, z, core), tp: 8 (over y_lo, x).
Axes of the slice: x: 4, y: 4 (y_hi: 2, y_lo: 2; y = y_hi * 2 + y_lo), z: 4, core: 2. Of those that a mesh axis runs over, the one named last changes fastest.
Arguments:
- queries: bfloat16 [16, 3, 512, 8192], P('pp', None, None, 'tp')
- attention_output_grads: bfloat16 [16, 3, 512, 8192], P('pp', None, None, 'tp'), may hold values from -6 to 6
- keys: bfloat16 [16, 3, 512, 1024], P('pp', None, None, 'tp')
- hidden: bfloat16 [16, 3, 512, 8192], P('pp', None, None, 'tp'), may hold values from -6 to 6
- value_weight: bfloat16 [16, 3, 8192, 1024], P('pp', None, 'tp'), may hold values from -0.1875 to 0.1875
- value_down_matrix: bfloat16 [16, 3, 8192, 64], P('pp', None, 'tp'), may hold values from -0.0625 to 0.0625
- value_up_matrix: bfloat16 [16, 3, 64, 1024], P('pp'), may hold values from -0.75 to 0.75
- document_index: int32 [512], replicated, may hold values from 0 to 7, never falling along the last dimension, each value on 1 to 256 neighbouring positions
- advantage: int32 [512], replicated, may hold values from -3 to 3
- loss_token_mask: int32 [512], replicated, may hold values 0 or 1
- top_stream_gradient: bfloat16 [512, 8192], P(None, 'tp'), may hold values from -6 to 6
Outputs:
- grad_in: bfloat16 [16, 3, 512, 8192], P('pp', None, None, 'tp')
- lora_a_grad: float32 [16, 3, 8192, 64], P('pp', None, 'tp')
- lora_b_grad: float32 [16, 3, 64, 1024], P('pp', None, None, 'tp')
All inputs are finite; a program needn't handle non-finite values.
Results may differ from a plain program's by a relative error of at most 0.019.
Values may be sent and summed in bfloat16 or wider, within the bound.
A program may use at most 448 MiB of HBM per device.

v0:
```python
import jax
import jax.numpy as jnp
from jax import lax
from jax.sharding import PartitionSpec as P

HD = 128
QPK = 8
SEGS = 8


adapter_scale = 2.0
epsilon = 1e-05


def prefix(x, axis, join, neutral):
    count = lax.axis_size(axis)
    place = lax.axis_index(axis)
    ahead = count - 1 - place
    gathered = lax.all_gather(x.astype(jnp.bfloat16), axis)
    state = jnp.zeros_like(x) + jnp.asarray(neutral, x.dtype)

    def one(lap, state):
        source = count - 1 - lap
        return join(state, lax.dynamic_index_in_dim(gathered, source, 0, False).astype(x.dtype))

    return lax.fori_loop(0, ahead, one, state)


def value_gradient(queries, keys, grads, document_index):
    total = keys.shape[0]
    groups = keys.shape[1] // HD
    block = min(512, total)
    key_heads = keys.reshape(total, groups, HD)
    positions = jnp.arange(total, dtype=jnp.int32)

    def one_block(carry, block_id):
        start = block_id * block
        query_block = queries.reshape(block, groups, QPK, HD)
        grad_block = grads.reshape(block, groups, QPK, HD)
        scores = jnp.einsum(
            "bgqh,kgh->gqbk", query_block, key_heads, preferred_element_type=jnp.float32
        ) * HD ** (-0.5)
        row_pos = start + jnp.arange(block, dtype=jnp.int32)
        allowed = (positions[None, :] <= row_pos[:, None]) & (
            document_index[None, :] == document_index[:, None]
        )
        scores = jnp.where(allowed, scores, -1e30)
        peak = jnp.max(scores, axis=-1, keepdims=True)
        expo = jnp.exp(scores - peak)
        weights = (expo / jnp.sum(expo, axis=-1, keepdims=True)).astype(jnp.bfloat16)
        return (
            carry
            + jnp.einsum("gqbk,bgqh->kgh", weights, grad_block, preferred_element_type=jnp.float32),
            None,
        )

    start_value = jnp.zeros((total, groups, HD), jnp.float32)
    result, unused = lax.scan(one_block, start_value, jnp.arange(total // block, dtype=jnp.int32))
    return result.reshape(total, groups * HD)


def add_sums(earlier_sum, later_sum):
    return earlier_sum + later_sum


def per_device(
    queries,
    attention_output_grads,
    keys,
    hidden,
    value_weight,
    value_down_matrix,
    value_up_matrix,
    document_index,
    advantage,
    loss_token_mask,
    top_stream_gradient,
):
    span_count = hidden.shape[1]
    local_width = hidden.shape[3]
    model_width = local_width * lax.axis_size("tp")
    all_tokens = document_index.shape[0]
    labels = jnp.arange(SEGS, dtype=jnp.int32)
    member = (document_index[:, None] == labels[None, :]).astype(jnp.float32)
    masked = loss_token_mask.astype(jnp.float32)
    counts = jnp.sum(member * masked[:, None], axis=0)
    inverse = 1.0 / jnp.maximum(counts, 1.0)
    per_token = jnp.sum(member * inverse[None, :], axis=1)
    token_weight = advantage.astype(jnp.float32) * masked * per_token * (all_tokens / SEGS)
    top_grad = token_weight[:, None] * top_stream_gradient.astype(jnp.float32)
    gradient_terms = []
    a_parts = []
    up_gradients = []
    for layer_in_section in range(span_count):
        value_stream_gradient = value_gradient(
            queries[0, layer_in_section],
            keys[0, layer_in_section],
            attention_output_grads[0, layer_in_section],
            document_index,
        ).astype(jnp.bfloat16)
        stream = hidden[0, layer_in_section].astype(jnp.float32)
        squares = lax.psum(jnp.sum(stream * stream, axis=1), "tp")
        inverse_rms = lax.rsqrt(squares / model_width + epsilon)
        normed = stream * inverse_rms[:, None]
        normalized_up = normed.astype(jnp.bfloat16)
        weight_rows = value_weight[0, layer_in_section]
        reduced_rows = value_down_matrix[0, layer_in_section]
        upward_matrix = value_up_matrix[0, layer_in_section]
        low_part = jnp.dot(normalized_up, reduced_rows, preferred_element_type=jnp.float32)
        piece = lax.all_gather(value_stream_gradient, "tp", axis=1, tiled=True)
        normalized_gradient = jnp.einsum(
            "tc,dc->td", piece, weight_rows, preferred_element_type=jnp.float32
        )
        adapter = jnp.einsum("tc,rc->tr", piece, upward_matrix, preferred_element_type=jnp.float32)
        adapter_upward = adapter.astype(jnp.bfloat16)
        normalized_gradient = normalized_gradient + adapter_scale * jnp.einsum(
            "tr,dr->td", adapter_upward, reduced_rows, preferred_element_type=jnp.float32
        )
        inner_part = jnp.sum(normed * normalized_gradient, axis=1)
        low_total, inner_total = (
            lax.psum(low_part.astype(jnp.bfloat16), "tp").astype(jnp.float32),
            lax.psum(inner_part.astype(jnp.bfloat16), "tp").astype(jnp.float32),
        )
        inner = (inner_total / model_width)[:, None]
        gradient_terms.append(
            (inverse_rms[:, None] * (normalized_gradient - normed * inner)).astype(jnp.bfloat16)
        )
        a_parts.append(
            adapter_scale
            * jnp.einsum(
                "td,tr->dr", normalized_up, adapter_upward, preferred_element_type=jnp.float32
            )
        )
        reduced_up = low_total.astype(jnp.bfloat16)
        up_gradients.append(
            adapter_scale
            * jnp.einsum(
                "tr,tc->rc", reduced_up, value_stream_gradient, preferred_element_type=jnp.float32
            )
        )
    stacked = jnp.stack(gradient_terms).astype(jnp.float32)
    above = prefix(stacked, "pp", add_sums, jnp.zeros_like(stacked))
    lap_totals = lax.psum(stacked[1:].astype(jnp.bfloat16), "pp").astype(jnp.float32)
    outputs = [top_grad for layer_in_section in range(span_count)]
    carried = top_grad
    for layer_in_section in reversed(range(span_count)):
        outputs[layer_in_section] = carried + above[layer_in_section] + stacked[layer_in_section]
        if layer_in_section > 0:
            carried = carried + lap_totals[layer_in_section - 1]
    grad_in = jnp.stack(outputs).astype(jnp.bfloat16)[None]
    return (grad_in, jnp.stack(a_parts)[None], jnp.stack(up_gradients)[None])


def solution(mesh):
    in_specs = (
        P("pp", None, None, "tp"),
        P("pp", None, None, "tp"),
        P("pp", None, None, "tp"),
        P("pp", None, None, "tp"),
        P("pp", None, "tp", None),
        P("pp", None, "tp", None),
        P("pp", None, None, None),
        P(),
        P(),
        P(),
        P(None, "tp"),
    )
    out_specs = (P("pp", None, None, "tp"), P("pp", None, "tp", None), P("pp", None, None, "tp"))
    return jax.shard_map(
        per_device, mesh=mesh, in_specs=in_specs, out_specs=out_specs, check_vma=False
    )
```

profile of v0, /device:TPU:1, one launch (start us, length us, event | category | flops | bytes accessed | tf_op | source)
XLA Modules:
  0.0 781.6 jit_solution(12804445285198296849)
XLA Ops:
  7.2 3.3 fusion.149
  10.5 1.3 copy.57
  12.0 3.5 fusion.150
  16.1 1.5 copy.60
  17.6 2.3 copy.58
  19.9 2.2 fusion.119
  22.1 3.2 fusion.5
  25.4 8.2 %fusion.2 = (f32[8,512]{1,0:T(8,128)S(1)}, f32[8,512]{1,0:T(8,128)S(1)}, f32[8,512]{1,0:T(8,128)S(1)}, f32[512,512,8]{1,0,2:T(8,128)}) fusion(f32[512,512,8]{1,0,2:T(8,128)S(1)} %get-tuple-element.165, f32[8,512]{1,0:T(8,128)S(1)} %get-tuple-element.132, pred[512,512]{0,1:T(8,128)(4,1)S(1)} %fusion.108, f32[8,512]{1,0:T(8,128)S(1)} %get-tuple-element.133, ...), kind=kOutput, calls=%fused_computation.12 | convolution fusion | flops 559927296 | bytes 26689536 | tf_op jit(solution)/shard_map/while/body/eval_jaxpr/bgqh,kgh->gqbk/dot_general | solution.py:40
  33.6 2.9 fusion.81
  37.3 5.3 fusion.1
  43.1 2.9 fusion.78
  46.1 1.3 copy.61
  47.4 6.6 fusion.75
  54.1 0.7 fusion.43
  54.8 18.0 %all-reduce = (f32[512]{0:T(512)}, f32[512]{0:T(512)}, f32[512]{0:T(512)}) all-reduce(f32[512]{0:T(512)S(1)} %get-tuple-element.126, f32[512]{0:T(512)S(1)} %get-tuple-element.127, f32[512]{0:T(512)S(1)} %get-tuple-element.128), channel_id=1, replica_groups=mesh['pp'=16,'tp'=8] {'tp'}, use_global_device_ids=true, to_apply=%region_16.17 | all-reduce | flops 1536 | bytes 12288 | tf_op jit(solution)/shard_map/psum | solution.py:102
  72.8 0.7 add_rsqrt_fusion.2
  73.5 0.7 add_rsqrt_fusion
  74.2 1.1 convolution_convert_fusion
  75.3 1.1 convolution_convert_fusion.1
  76.5 1.1 convolution_convert_fusion.2
  78.0 3.3 fusion.58
  82.2 31.9 %all-gather.8.cloned.1.call-done = bf16[512,1024]{1,0:T(8,128)(2,1)} async-done(((bf16[512,128]{1,0:T(8,128)(2,1)}), bf16[512,1024]{1,0:T(8,128)(2,1)}) %all-gather.8.cloned.1.call-update) | async-done | bytes 1048592 | tf_op jit(solution)/shard_map/all_gather | solution.py:110
  114.1 3.3 fusion.56
  117.9 1.8 multiply_add_fusion.1
  119.6 35.0 %all-gather.10.cloned.1.call-done = bf16[512,1024]{1,0:T(8,128)(2,1)} async-done(((bf16[512,128]{1,0:T(8,128)(2,1)}), bf16[512,1024]{1,0:T(8,128)(2,1)}) %all-gather.10.cloned.1.call-update) | async-done | bytes 1048592 | tf_op jit(solution)/shard_map/all_gather | solution.py:110
  154.6 3.3 fusion.54
  158.5 3.8 fusion.39
  162.3 14.9 %all-reduce.1 = (bf16[512]{0:T(512)(128)(2,1)S(1)}, bf16[512]{0:T(512)(128)(2,1)S(1)}, bf16[512]{0:T(512)(128)(2,1)S(1)}) all-reduce(bf16[512]{0:T(512)(128)(2,1)S(1)} %get-tuple-element.125, bf16[512]{0:T(512)(128)(2,1)S(1)} %get-tuple-element.124, bf16[512]{0:T(512)(128)(2,1)S(1)} %get-tuple-element.123), channel_id=1, replica_groups=mesh['pp'=16,'tp'=8] {'tp'}, use_global_device_ids=true, to_apply=%region_13.14 | all-reduce | flops 1536 | bytes 6144 | tf_op jit(solution)/shard_map/psum | solution.py:122
  177.1 4.6 fusion.91
  181.7 1.0 copy-done.3
  182.7 1.5 pad_maximum_fusion.2
  184.3 5.0 pad_maximum_fusion
  189.4 1.4 convert_element_type.159
  190.8 0.8 select_reduce_fusion.1
  191.7 0.7 multiply_multiply_fusion
  192.4 39.4 %all-reduce.8.cloned.1.call-done = (bf16[512,64]{0,1:T(8,128)(2,1)}, bf16[512,64]{0,1:T(8,128)(2,1)}, bf16[512,64]{0,1:T(8,128)(2,1)}) async-done(((bf16[512,64]{0,1:T(8,128)(2,1)}, bf16[512,64]{0,1:T(8,128)(2,1)}, bf16[512,64]{0,1:T(8,128)(2,1)}), (bf16[512,64]{0,1:T(8,128)(2,1)}, bf16[512,64]{0,1:T(8,128)(2,1)}, bf16[512,64]{0,1:T(8,128)(2,1)})) %all-reduce.8.cloned.1.call-update) | async-done | bytes 196624 | tf_op jit(solution)/shard_map/psum | solution.py:121
  231.8 1.0 fusion.84
  232.8 1.0 fusion.85
  233.8 1.0 fusion.86
  234.8 0.7 maximum_bitcast_fusion.1
  235.5 1.3 fusion.72
  236.8 1.3 fusion.73
  238.5 0.9 maximum_bitcast_fusion
  239.4 143.8 %all-reduce.6.cloned.1.call-done = bf16[2,512,1024]{2,1,0:T(8,128)(2,1)} async-done(((bf16[2,512,1024]{2,1,0:T(8,128)(2,1)}), bf16[2,512,1024]{2,1,0:T(8,128)(2,1)}) %all-reduce.6.cloned.1.call-update) | async-done | bytes 2097168 | tf_op jit(solution)/shard_map/psum | solution.py:143
  383.2 4.0 convert_element_type.177
  387.1 263.8 %all-gather.12.cloned.1.call-done = bf16[48,512,1024]{2,1,0:T(8,128)(2,1)} async-done(((bf16[3,512,1024]{2,1,0:T(8,128)(2,1)}), bf16[48,512,1024]{2,1,0:T(8,128)(2,1)}) %all-gather.12.cloned.1.call-update) | async-done | bytes 50331664 | tf_op jit(solution)/shard_map/all_gather | solution.py:19
  651.0 3.4 broadcast_in_dim.80
  654.4 111.4 %while.8 = (s32[]{:T(128)}, f32[3,512,1024]{2,1,0:T(8,128)}, s32[]{:T(128)}, bf16[16,3,512,1024]{3,2,1,0:T(8,128)(2,1)}, s32[]{:T(128)}, /*index=5*/s32[]{:T(128)}, s32[]{:T(128)}, s32[]{:T(128)}) while((s32[]{:T(128)}, f32[3,512,1024]{2,1,0:T(8,128)}, s32[]{:T(128)}, bf16[16,3,512,1024]{3,2,1,0:T(8,128)(2,1)}, s32[]{:T(128)}, ...), condition=%wide.region_22.23_spmd, body=%wide.region_21.22_spmd.sunk | while | flops 3145734 | bytes 15728783 | solution.py:26
  654.4 8.0 %convert_add_fusion.2 = f32[3,512,1024]{2,1,0:T(8,128)} fusion(f32[3,512,1024]{2,1,0:T(8,128)} %get-tuple-element.205, bf16[16,3,512,1024]{3,2,1,0:T(8,128)(2,1)} %get-tuple-element.215, s32[]{:T(128)S(6)} %select_n.66), kind=kLoop, calls=%fused_computation.clone.1 | loop fusion | flops 3145728 | bytes 15728644 | tf_op jit(solution)/shard_map/while/body/add | solution.py:63
  662.4 8.0 %convert_add_fusion.2 = f32[3,512,1024]{2,1,0:T(8,128)} fusion(f32[3,512,1024]{2,1,0:T(8,128)} %get-tuple-element.205, bf16[16,3,512,1024]{3,2,1,0:T(8,128)(2,1)} %get-tuple-element.215, s32[]{:T(128)S(6)} %select_n.66), kind=kLoop, calls=%fused_computation.clone.1 | loop fusion | flops 3145728 | bytes 15728644 | tf_op jit(solution)/shard_map/while/body/add | solution.py:63
  670.3 8.0 %convert_add_fusion.2 = f32[3,512,1024]{2,1,0:T(8,128)} fusion(f32[3,512,1024]{2,1,0:T(8,128)} %get-tuple-element.205, bf16[16,3,512,1024]{3,2,1,0:T(8,128)(2,1)} %get-tuple-element.215, s32[]{:T(128)S(6)} %select_n.66), kind=kLoop, calls=%fused_computation.clone.1 | loop fusion | flops 3145728 | bytes 15728644 | tf_op jit(solution)/shard_map/while/body/add | solution.py:63
  678.3 8.0 %convert_add_fusion.2 = f32[3,512,1024]{2,1,0:T(8,128)} fusion(f32[3,512,1024]{2,1,0:T(8,128)} %get-tuple-element.205, bf16[16,3,512,1024]{3,2,1,0:T(8,128)(2,1)} %get-tuple-element.215, s32[]{:T(128)S(6)} %select_n.66), kind=kLoop, calls=%fused_computation.clone.1 | loop fusion | flops 3145728 | bytes 15728644 | tf_op jit(solution)/shard_map/while/body/add | solution.py:63
  686.2 8.0 %convert_add_fusion.2 = f32[3,512,1024]{2,1,0:T(8,128)} fusion(f32[3,512,1024]{2,1,0:T(8,128)} %get-tuple-element.205, bf16[16,3,512,1024]{3,2,1,0:T(8,128)(2,1)} %get-tuple-element.215, s32[]{:T(128)S(6)} %select_n.66), kind=kLoop, calls=%fused_computation.clone.1 | loop fusion | flops 3145728 | bytes 15728644 | tf_op jit(solution)/shard_map/while/body/add | solution.py:63
  694.2 8.0 %convert_add_fusion.2 = f32[3,512,1024]{2,1,0:T(8,128)} fusion(f32[3,512,1024]{2,1,0:T(8,128)} %get-tuple-element.205, bf16[16,3,512,1024]{3,2,1,0:T(8,128)(2,1)} %get-tuple-element.215, s32[]{:T(128)S(6)} %select_n.66), kind=kLoop, calls=%fused_computation.clone.1 | loop fusion | flops 3145728 | bytes 15728644 | tf_op jit(solution)/shard_map/while/body/add | solution.py:63
  702.1 8.0 %convert_add_fusion.2 = f32[3,512,1024]{2,1,0:T(8,128)} fusion(f32[3,512,1024]{2,1,0:T(8,128)} %get-tuple-element.205, bf16[16,3,512,1024]{3,2,1,0:T(8,128)(2,1)} %get-tuple-element.215, s32[]{:T(128)S(6)} %select_n.66), kind=kLoop, calls=%fused_computation.clone.1 | loop fusion | flops 3145728 | bytes 15728644 | tf_op jit(solution)/shard_map/while/body/add | solution.py:63
  710.1 8.0 %convert_add_fusion.2 = f32[3,512,1024]{2,1,0:T(8,128)} fusion(f32[3,512,1024]{2,1,0:T(8,128)} %get-tuple-element.205, bf16[16,3,512,1024]{3,2,1,0:T(8,128)(2,1)} %get-tuple-element.215, s32[]{:T(128)S(6)} %select_n.66), kind=kLoop, calls=%fused_computation.clone.1 | loop fusion | flops 3145728 | bytes 15728644 | tf_op jit(solution)/shard_map/while/body/add | solution.py:63
  718.0 8.0 %convert_add_fusion.2 = f32[3,512,1024]{2,1,0:T(8,128)} fusion(f32[3,512,1024]{2,1,0:T(8,128)} %get-tuple-element.205, bf16[16,3,512,1024]{3,2,1,0:T(8,128)(2,1)} %get-tuple-element.215, s32[]{:T(128)S(6)} %select_n.66), kind=kLoop, calls=%fused_computation.clone.1 | loop fusion | flops 3145728 | bytes 15728644 | tf_op jit(solution)/shard_map/while/body/add | solution.py:63
  726.0 8.0 %convert_add_fusion.2 = f32[3,512,1024]{2,1,0:T(8,128)} fusion(f32[3,512,1024]{2,1,0:T(8,128)} %get-tuple-element.205, bf16[16,3,512,1024]{3,2,1,0:T(8,128)(2,1)} %get-tuple-element.215, s32[]{:T(128)S(6)} %select_n.66), kind=kLoop, calls=%fused_computation.clone.1 | loop fusion | flops 3145728 | bytes 15728644 | tf_op jit(solution)/shard_map/while/body/add | solution.py:63
  733.9 8.0 %convert_add_fusion.2 = f32[3,512,1024]{2,1,0:T(8,128)} fusion(f32[3,512,1024]{2,1,0:T(8,128)} %get-tuple-element.205, bf16[16,3,512,1024]{3,2,1,0:T(8,128)(2,1)} %get-tuple-element.215, s32[]{:T(128)S(6)} %select_n.66), kind=kLoop, calls=%fused_computation.clone.1 | loop fusion | flops 3145728 | bytes 15728644 | tf_op jit(solution)/shard_map/while/body/add | solution.py:63
  741.9 8.0 %convert_add_fusion.2 = f32[3,512,1024]{2,1,0:T(8,128)} fusion(f32[3,512,1024]{2,1,0:T(8,128)} %get-tuple-element.205, bf16[16,3,512,1024]{3,2,1,0:T(8,128)(2,1)} %get-tuple-element.215, s32[]{:T(128)S(6)} %select_n.66), kind=kLoop, calls=%fused_computation.clone.1 | loop fusion | flops 3145728 | bytes 15728644 | tf_op jit(solution)/shard_map/while/body/add | solution.py:63
  749.8 8.0 %convert_add_fusion.2 = f32[3,512,1024]{2,1,0:T(8,128)} fusion(f32[3,512,1024]{2,1,0:T(8,128)} %get-tuple-element.205, bf16[16,3,512,1024]{3,2,1,0:T(8,128)(2,1)} %get-tuple-element.215, s32[]{:T(128)S(6)} %select_n.66), kind=kLoop, calls=%fused_computation.clone.1 | loop fusion | flops 3145728 | bytes 15728644 | tf_op jit(solution)/shard_map/while/body/add | solution.py:63
  757.8 8.0 %convert_add_fusion.2 = f32[3,512,1024]{2,1,0:T(8,128)} fusion(f32[3,512,1024]{2,1,0:T(8,128)} %get-tuple-element.205, bf16[16,3,512,1024]{3,2,1,0:T(8,128)(2,1)} %get-tuple-element.215, s32[]{:T(128)S(6)} %select_n.66), kind=kLoop, calls=%fused_computation.clone.1 | loop fusion | flops 3145728 | bytes 15728644 | tf_op jit(solution)/shard_map/while/body/add | solution.py:63
  765.8 7.0 fusion.107
  772.8 2.0 pad_maximum_fusion.1
  (75 shorter events, 4.9 us)
Async XLA Ops:
  7.2 4.6 copy-start.24
  7.2 70.8 %all-gather.6.cloned.1.call-start = ((), (), s32[]{:S(2)}) async-start(), calls=%async_computation | async-start | bytes 1179648 | tf_op jit(solution)/shard_map/all_gather | solution.py:110
  19.9 2.2 copy-start.23
  22.1 3.2 copy-start.12
  25.3 8.3 %copy-start.4 = (f32[512,512,8]{1,0,2:T(8,128)}, f32[512,512,8]{1,0,2:T(8,128)S(1)}, u32[]{:S(2)}) copy-start(f32[512,512,8]{1,0,2:T(8,128)S(1)} %get-tuple-element.165) | copy-start | bytes 25165828
  25.4 8.2 %copy-start.11 = (bf16[1,1,512,1024]{2,3,1,0:T(8,128)(2,1)S(1)}, bf16[1,1,512,1024]{2,3,1,0:T(8,128)(2,1)}, u32[]{:S(2)}) copy-start(bf16[1,1,512,1024]{2,3,1,0:T(8,128)(2,1)} %copy.57) | copy-start | bytes 3145732
  33.6 3.2 copy-start.7
  36.5 77.6 %all-gather.8.cloned.1.call-start = ((), (), s32[]{:S(2)}) async-start(), calls=%async_computation.1 | async-start | bytes 1179648 | tf_op jit(solution)/shard_map/all_gather | solution.py:110
  37.3 5.8 copy-start.5
  46.0 108.6 %all-gather.10.cloned.1.call-start = ((), (), s32[]{:S(2)}) async-start(), calls=%async_computation.3 | async-start | bytes 1179648 | tf_op jit(solution)/shard_map/all_gather | solution.py:110
  47.4 6.7 copy-start.1
  54.0 20.2 %copy-start.17 = (bf16[1,3,1024,64]{2,3,1,0:T(8,128)(2,1)S(1)}, bf16[1,3,1024,64]{2,3,1,0:T(8,128)(2,1)}, u32[]{:S(2)}) copy-start(bf16[1,3,1024,64]{2,3,1,0:T(8,128)(2,1)} %param.18) | copy-start | bytes 1179652
  54.0 177.8 %all-reduce.8.cloned.1.call-start = ((), (), s32[]{:S(2)}) async-start(), calls=%async_computation.5 | async-start | bytes 393216 | tf_op jit(solution)/shard_map/psum | solution.py:121
  77.6 3.6 copy-start.18
  77.6 305.5 %all-reduce.6.cloned.1.call-start = ((), (), s32[]{:S(2)}) async-start(), calls=%async_computation.2 | async-start | bytes 4194304 | tf_op jit(solution)/shard_map/psum | solution.py:143
  77.9 3.3 copy-start.8
  81.7 35.7 %copy-start.19 = (bf16[512,64]{0,1:T(8,128)(2,1)}, bf16[512,64]{0,1:T(8,128)(2,1)S(1)}, u32[]{:S(2)}) copy-start(bf16[512,64]{0,1:T(8,128)(2,1)S(1)} %convolution_convert_fusion.5) | copy-start | bytes 196612
  114.1 3.3 copy-start.9
  117.8 40.1 %copy-start.20 = (bf16[512,64]{0,1:T(8,128)(2,1)}, bf16[512,64]{0,1:T(8,128)(2,1)S(1)}, u32[]{:S(2)}) copy-start(bf16[512,64]{0,1:T(8,128)(2,1)S(1)} %convolution_convert_fusion.4) | copy-start | bytes 196612
  154.6 3.4 copy-start.10
  154.6 3.8 copy-start
  158.5 3.8 copy-start.21
  181.7 1.0 copy-start.3
  182.7 1.6 copy-start.6
  184.2 466.7 %all-gather.12.cloned.1.call-start = ((), (), s32[]{:S(2)}) async-start(), calls=%async_computation.4 | async-start | bytes 53477376 | tf_op jit(solution)/shard_map/all_gather | solution.py:19
  184.3 47.5 %copy-start.15 = (bf16[512,128]{1,0:T(8,128)(2,1)S(1)}, bf16[512,128]{1,0:T(8,128)(2,1)}, u32[]{:S(2)}) copy-start(bf16[512,128]{1,0:T(8,128)(2,1)} %fusion.78) | copy-start | bytes 393220
  189.3 43.5 %copy-start.14 = (bf16[512,128]{1,0:T(8,128)(2,1)S(1)}, bf16[512,128]{1,0:T(8,128)(2,1)}, u32[]{:S(2)}) copy-start(bf16[512,128]{1,0:T(8,128)(2,1)} %fusion.81) | copy-start | bytes 393220
  189.3 44.5 %copy-start.16 = (bf16[512,128]{1,0:T(8,128)(2,1)S(1)}, bf16[512,128]{1,0:T(8,128)(2,1)}, u32[]{:S(2)}) copy-start(bf16[512,128]{1,0:T(8,128)(2,1)} %fusion.75) | copy-start | bytes 393220
  189.3 46.2 %copy-start.2 = (bf16[1,3,512,1024]{3,2,1,0:T(8,128)(2,1)S(1)}, bf16[1,3,512,1024]{3,2,1,0:T(8,128)(2,1)}, u32[]{:S(2)}) copy-start(bf16[1,3,512,1024]{3,2,1,0:T(8,128)(2,1)} %param.16) | copy-start | bytes 9437188
  231.8 6.2 copy-start.22
  654.4 111.4 %copy-start.13 = (bf16[512,1024]{1,0:T(8,128)(2,1)S(1)}, bf16[512,1024]{1,0:T(8,128)(2,1)}, u32[]{:S(2)}) copy-start(bf16[512,1024]{1,0:T(8,128)(2,1)} %param.23) | copy-start | bytes 3145732
Sparse Core Ops, SparseCore 0:
  36.7 36.7 all-gather.5
  75.0 39.0 all-gather.7
  115.7 38.9 all-gather.9
  157.7 74.0 all-reduce.7
  234.3 148.7 all-reduce.5
  386.4 264.5 all-gather.11
where the time goes:
time: 789 us; the launch traced here: 782 us
  waiting for transfers between devices  514 us (65%)
  other arithmetic  148 us (19%)
  matrix products  52.6 us (7%)
  blocking collectives  32.9 us (4%)
  local copies, waits for them, and re-layouts  19.2 us (2%)
  between operations  14.5 us (2%)
    all_gather x1, waiting for transfers between devices, prefix(): gathered = lax.all_gather(x.astype(jnp.bfloat16), axis)  264 us
    psum x1, waiting for transfers between devices, per_device(): lax.psum(stacked[1:].astype(jnp.bfloat16), 'pp').astype(jnp.float32)  144 us
    add x14, other arithmetic, add_sums(): return earlier_sum + later_sum  111 us
    all_gather x3, waiting for transfers between devices, per_device(): piece = lax.all_gather(value_stream_gradient, 'tp', axis=1, tiled=True)  67 us
    psum x1, waiting for transfers between devices, per_device(): lax.psum(low_part.astype(jnp.bfloat16), 'tp').astype(jnp.float32)  39.4 us
    psum x1, blocking collectives, per_device(): squares = lax.psum(jnp.sum(stream * stream, axis=1), 'tp')  18 us
  transfers between devices with their start and end apart: 6, of which 5 were waited for; matrix products, arithmetic and copies ran while one was open for 8% of the time, Pallas kernels for 0%

commit v1 on v0

v1 whole, which is shorter than its diff:
```python
import jax
import jax.numpy as jnp
from jax import lax
from jax.experimental import pallas as pl
from jax.experimental.pallas import tpu as pltpu
from jax.sharding import PartitionSpec as P

MESH = pl.DeviceIdType.MESH
BF16 = jnp.bfloat16
F32 = jnp.float32
LAYERS = 3
TOKENS = 512
WIDTH = 1024
HEAD = 128
HEADS = 8
RANK = 64
HALF = 256
ROWS = 32
CHIPS = 8
TP = 8
MODEL = 8192
SEGS = 8
LOG2E = 1.4426950408889634
SOFTMAX_SCALE = HEAD**-0.5 * LOG2E
MASK_OFFSET = (0, 128, 384, 768)


def dot(a, b, dims):
    return lax.dot_general(a, b, (dims, ((), ())), preferred_element_type=F32)


def kernel(
    q_hbm, g_hbm, k_hbm, h_hbm, w_hbm, dn_hbm, up_hbm, top_hbm, doc_ref, adv_ref, loss_ref,
    out_hbm, la_hbm, lb_hbm,
    q_v, g_v, k_v, h_v, w_v, dn_v, up_v, top_v,
    mask_v, weight_v, acc_v, vg_v, hd_v, ad_v, ng_v, inv_v,
    sqs_v, sqr_v, ins_v, inr_v, lbs_v, lbr_v, la_v, lb_v,
    t_v, tp_v, p_v, q8_v, rs_v, rr_v, carry_v, own_v, peer_v,
    in_sem, out_sem,
    gs_sem, gr_sem, sqs_sem, sqr_sem, ins_sem, inr_sem, lbs_sem, lbr_sem,
    cs_sem, cr_sem, p1s_sem, p1r_sem, p2s_sem, p2r_sem, os_sem, or_sem,
):
    pp = lax.axis_index("pp")
    tp = lax.axis_index("tp")
    core = lax.rem(pp, 2)
    chip = lax.div(pp, 2)
    yl = lax.div(tp, 4)
    x = lax.rem(tp, 4)

    yl_peer = (pp, (1 - yl) * 4 + x)
    x_up = (pp, yl * 4 + lax.rem(x + 1, 4))
    x_down = (pp, yl * 4 + lax.rem(x + 3, 4))
    core_peer = (chip * 2 + (1 - core), tp)

    def tp_peer(j):
        return (pp, lax.rem(tp + j, TP))

    def chip_index(j):
        return lax.rem(chip + j, CHIPS)

    def chip_peer(j):
        return (chip_index(j) * 2 + core, tp)

    copies = {}

    def load(name, index, src, dst):
        copies[name] = pltpu.make_async_copy(src, dst, in_sem.at[index])
        copies[name].start()

    count = 0
    for l in (2, 1, 0):
        for name, src, dst in (("k", k_hbm, k_v), ("q", q_hbm, q_v), ("g", g_hbm, g_v)):
            load((name, l), count, src.at[l], dst.at[l])
            count += 1
        if l == 2:
            load("h", count, h_hbm, h_v)
            load("dn", count + 1, dn_hbm, dn_v)
            load("up", count + 2, up_hbm, up_v)
            count += 3
    for l in (2, 1, 0):
        load(("w", l), count, w_hbm.at[l], w_v.at[l])
        count += 1
    own_row = core * HALF + chip * ROWS
    load("top", count, top_hbm.at[pl.ds(pl.multiple_of(own_row, ROWS), ROWS)], top_v)

    barrier = pltpu.get_barrier_semaphore()
    for j in range(1, TP):
        pl.semaphore_signal(barrier, inc=1, device_id=tp_peer(j), device_id_type=MESH)
    for j in range(1, CHIPS):
        pl.semaphore_signal(barrier, inc=1, device_id=chip_peer(j), device_id_type=MESH)
    pl.semaphore_signal(barrier, inc=1, device_id=core_peer, device_id_type=MESH)

    def remote(src, dst, send, recv, device):
        return pltpu.make_async_remote_copy(
            src_ref=src, dst_ref=dst, send_sem=send, recv_sem=recv, device_id=device, device_id_type=MESH
        )

    def columns(row):
        return jnp.transpose(jnp.broadcast_to(row, (128, TOKENS)))

    def rows_of(sums):
        return jnp.sum(jnp.transpose(sums), axis=0, keepdims=True)

    doc_row = doc_ref[...].astype(F32)
    doc_col = columns(doc_row)
    key_pos = lax.broadcasted_iota(jnp.int32, (128, 128), 0)
    query_pos = lax.broadcasted_iota(jnp.int32, (128, 128), 1)
    for b in range(4):
        low = max(0, b - 2)
        for kb in range(low, b + 1):
            allowed = doc_col[128 * kb : 128 * kb + 128, :] == doc_row[:, 128 * b : 128 * b + 128]
            if kb == b:
                allowed = allowed & (key_pos <= query_pos)
            at = MASK_OFFSET[b] + 128 * (kb - low)
            mask_v[at : at + 128, :] = jnp.where(allowed, 0.0, -jnp.inf)
    loss_row = loss_ref[...].astype(F32)
    labels = lax.broadcasted_iota(jnp.int32, (SEGS, TOKENS), 0).astype(F32)
    member = jnp.where(labels == doc_row, 1.0, 0.0)
    counts = jnp.sum(member * loss_row, axis=1, keepdims=True)
    per_token = jnp.sum(member * (1.0 / jnp.maximum(counts, 1.0)), axis=0, keepdims=True)
    weight_v[...] = columns(adv_ref[...].astype(F32) * loss_row * per_token * (TOKENS / SEGS))

    slot = x * 2 + yl
    other = x * 2 + (1 - yl)
    left = lax.rem(x + 3, 4) * 2
    right = lax.rem(x + 1, 4) * 2
    across = lax.rem(x + 2, 4) * 2

    def attention(l):
        for name in ("k", "q", "g"):
            copies[(name, l)].wait()
        for b in range(4):
            low, high = max(0, b - 2) * 128, (b + 1) * 128
            keys = k_v[l, low:high, :]
            mask = mask_v[MASK_OFFSET[b] : MASK_OFFSET[b] + high - low, :]
            mask4 = jnp.concatenate([mask] * 4, axis=1)
            total = None
            for part in range(2):
                heads = range(4 * part, 4 * part + 4)
                block = slice(128 * b, 128 * b + 128)
                queries = jnp.concatenate([q_v[l, block, HEAD * i : HEAD * i + HEAD] for i in heads], axis=0)
                grads = jnp.concatenate([g_v[l, block, HEAD * i : HEAD * i + HEAD] for i in heads], axis=0)
                scores = dot(keys, queries, ((1,), (1,))) + mask4
                peak = jnp.max(scores, axis=0, keepdims=True)
                expo = jnp.exp2((scores - peak) * SOFTMAX_SCALE)
                probs = (expo * (1.0 / jnp.sum(expo, axis=0, keepdims=True))).astype(BF16)
                piece = dot(probs, grads, ((1,), (0,)))
                total = piece if total is None else total + piece
            if b == 0:
                acc_v[0:128, :] = total
            else:
                acc_v[low : high - 128, :] += total[: high - low - 128]
                acc_v[high - 128 : high, :] = total[high - low - 128 :]
        vg_v[l, slot] = acc_v[...].astype(BF16)

    def gather_copy(l, i, place, device):
        return remote(vg_v.at[l, place], vg_v.at[l, place], gs_sem.at[l, i], gr_sem.at[l, i], device)

    def gather_out(l, i):
        return (
            lambda: gather_copy(l, 0, slot, yl_peer),
            lambda: gather_copy(l, 1, slot, x_up),
            lambda: gather_copy(l, 2, slot, x_down),
            lambda: gather_copy(l, 3, other, x_up),
            lambda: gather_copy(l, 4, other, x_down),
            lambda: gather_copy(l, 5, left + yl, x_up),
            lambda: gather_copy(l, 6, right + (1 - yl), x_down),
        )[i]()

    def gather_in(l, i):
        place = (other, left + yl, right + yl, left + (1 - yl), right + (1 - yl), across + yl, across + (1 - yl))[i]
        return gather_copy(l, i, place, yl_peer)

    def gather_1(l):
        for i in (0, 1, 2):
            gather_out(l, i).start()

    def gather_2(l):
        gather_in(l, 0).wait_recv()
        for i in (3, 4):
            gather_out(l, i).start()

    def gather_3(l):
        gather_in(l, 1).wait_recv()
        gather_out(l, 5).start()
        gather_in(l, 4).wait_recv()
        gather_out(l, 6).start()

    def gather_end(l):
        for i in (2, 3, 5, 6):
            gather_in(l, i).wait_recv()

    def squares_and_low():
        sqs_v[...] = jnp.zeros((8, TOKENS), F32)
        copies["h"].wait()
        copies["dn"].wait()
        for l in range(LAYERS):
            sums = None
            for n in range(WIDTH // 128):
                part = h_v[l, :, 128 * n : 128 * n + 128].astype(F32)
                sums = part * part if sums is None else sums + part * part
            sqs_v[l : l + 1, :] = rows_of(sums)
            hd_v[l] = dot(h_v[l], dn_v[l], ((1,), (0,)))
        sqr_v[tp] = sqs_v[...]

    def squares_copy(j, place):
        return remote(sqs_v, sqr_v.at[place], sqs_sem.at[j - 1], sqr_sem.at[j - 1], tp_peer(j))

    def squares_send():
        for j in range(1, TP):
            squares_copy(j, tp).start()

    def squares_wait():
        for j in range(1, TP):
            squares_copy(j, lax.rem(tp - j + TP, TP)).wait_recv()
        total = sqr_v[0]
        for i in range(1, TP):
            total = total + sqr_v[i]
        inverse = lax.rsqrt(total * (1.0 / MODEL) + 1e-5)
        for l in range(LAYERS):
            inv_v[l] = columns(inverse[l : l + 1, :])

    def gathered(l):
        return jnp.concatenate([vg_v[l, (j % 4) * 2 + j // 4] for j in range(TP)], axis=1)

    def inner_copy(l, j, place):
        return remote(ins_v.at[l], inr_v.at[l, place], ins_sem.at[l, j - 1], inr_sem.at[l, j - 1], tp_peer(j))

    def products(l):
        if l == 2:
            copies["up"].wait()
        copies[("w", l)].wait()
        ad_v[l] = dot(gathered(l), up_v[l], ((1,), (1,))).astype(BF16)
        acc_v[...] = jnp.zeros((TOKENS, 128), F32)

        def one(n, unused):
            start = pl.multiple_of(n * 256, 256)
            rows = pl.ds(start, 256)
            twice = (ad_v[l].astype(F32) * 2.0).astype(BF16)
            ng = dot(gathered(l), w_v[l, rows, :], ((1,), (1,))) + dot(twice, dn_v[l, rows, :], ((1,), (1,)))
            ng_v[:, rows] = ng
            prod = h_v[l, :, rows].astype(F32) * ng
            acc_v[...] += prod[:, :128] + prod[:, 128:]
            return unused

        lax.fori_loop(0, WIDTH // 256, one, 0)
        ins_v[l] = jnp.broadcast_to(rows_of(acc_v[...]), (8, TOKENS))
        inr_v[l, tp] = ins_v[l]
        for j in range(1, TP):
            inner_copy(l, j, tp).start()

    def terms(l):
        for j in range(1, TP):
            inner_copy(l, j, lax.rem(tp - j + TP, TP)).wait_recv()
        total = inr_v[l, 0]
        for i in range(1, TP):
            total = total + inr_v[l, i]
        inv = inv_v[l]
        acc_v[...] = inv * inv * inv * columns(total[0:1, :]) * (1.0 / MODEL)

        def one(n, unused):
            cols = pl.ds(pl.multiple_of(n * 128, 128), 128)
            t_v[l, :, cols] = (inv_v[l] * ng_v[:, cols] - acc_v[...] * h_v[l, :, cols].astype(F32)).astype(BF16)
            return unused

        lax.fori_loop(0, WIDTH // 128, one, 0)

    def lora_b_copy(l, j, block, place):
        return remote(lbs_v.at[l, block], lbr_v.at[l, place], lbs_sem.at[l, j - 1], lbr_sem.at[l, j - 1], tp_peer(j))

    def adapters(l):
        inv = inv_v[l][:, :RANK]
        scaled = (2.0 * inv * ad_v[l].astype(F32)).astype(BF16)
        la_v[l] = jnp.transpose(dot(scaled, h_v[l], ((0,), (0,))))
        low = (2.0 * inv * hd_v[l]).astype(BF16)
        part = dot(low, gathered(l), ((0,), (0,)))
        for j in range(TP):
            lbs_v[l, j] = part[:, 128 * j : 128 * j + 128].astype(BF16)
        lbr_v[l, tp] = lbs_v[l, tp]
        for j in range(1, TP):
            lora_b_copy(l, j, lax.rem(tp + j, TP), tp).start()
        pltpu.make_async_copy(la_v.at[l], la_hbm.at[l], out_sem.at[l]).start()

    def adapters_end(l):
        for j in range(1, TP):
            lora_b_copy(l, j, 0, lax.rem(tp - j + TP, TP)).wait_recv()
        total = lbr_v[l, 0].astype(F32)
        for i in range(1, TP):
            total = total + lbr_v[l, i].astype(F32)
        lb_v[l] = total
        pltpu.make_async_copy(lb_v.at[l], lb_hbm.at[l], out_sem.at[LAYERS + l]).start()

    mine = pl.ds(pl.multiple_of(core * HALF, HALF), HALF)
    theirs = pl.ds(pl.multiple_of((1 - core) * HALF, HALF), HALF)

    def core_copy(l):
        return remote(t_v.at[l, theirs], tp_v.at[l], cs_sem.at[l], cr_sem.at[l], core_peer)

    def block(i):
        return pl.ds(pl.multiple_of(i * ROWS, ROWS), ROWS)

    def to_owner(l, j, place):
        return remote(p_v.at[l, block(chip_index(j))], q8_v.at[l, place], p1s_sem.at[l, j - 1], p1r_sem.at[l, j - 1], chip_peer(j))

    def from_owner(l, j, place):
        return remote(rs_v.at[l, chip_index(j)], rr_v.at[l, block(place)], p2s_sem.at[l, j - 1], p2r_sem.at[l, j - 1], chip_peer(j))

    def source(j):
        return lax.rem(chip - j + CHIPS, CHIPS)

    def pair_sums(l):
        core_copy(l).wait_recv()
        p_v[l] = (t_v[l, mine, :].astype(F32) + tp_v[l].astype(F32)).astype(BF16)
        for j in (4, 2, 6, 1, 3, 5, 7):
            to_owner(l, j, chip).start()
        q8_v[l, chip] = p_v[l, block(chip), :]

    def suffix(l):
        if l == LAYERS - 1:
            copies["top"].wait()
            weight = weight_v[pl.ds(pl.multiple_of(own_row, ROWS), ROWS), :]
            weights = jnp.concatenate([weight] * (WIDTH // 128), axis=1)
            carry = weights * top_v[...].astype(F32)
        else:
            carry = carry_v[...]
        for j in range(1, CHIPS):
            to_owner(l, j, source(j)).wait_recv()
        for i in reversed(range(CHIPS)):
            rs_v[l, i] = carry.astype(BF16)
            carry = carry + q8_v[l, i].astype(F32)
        carry_v[...] = carry
        for j in (4, 2, 6, 1, 3, 5, 7):
            from_owner(l, j, chip).start()
        rr_v[l, block(chip), :] = rs_v[l, chip]

    def out_copy(l):
        return remote(peer_v.at[l], out_hbm.at[l, mine], os_sem.at[l], or_sem.at[l], core_peer)

    def out_here(l):
        return pltpu.make_async_copy(own_v.at[l], out_hbm.at[l, mine], out_sem.at[2 * LAYERS + l])

    def finish(l):
        for j in range(1, CHIPS):
            from_owner(l, j, source(j)).wait_recv()
        first = (1 - core).astype(F32)
        second = core.astype(F32)
        carry = rr_v[l].astype(F32)
        term = t_v[l, mine, :].astype(F32)
        peer_term = tp_v[l].astype(F32)
        peer_v[l] = (carry + peer_term + second * term).astype(BF16)
        out_copy(l).start()
        own_v[l] = (carry + term + first * peer_term).astype(BF16)
        out_here(l).start()

    attention(2)
    pl.semaphore_wait(barrier, TP + CHIPS - 1)
    gather_1(2)
    squares_and_low()
    squares_send()
    gather_2(2)
    attention(1)
    gather_3(2)
    gather_1(1)
    attention(0)
    gather_2(1)
    squares_wait()
    gather_end(2)
    products(2)
    gather_3(1)
    gather_1(0)
    adapters(2)
    terms(2)
    core_copy(2).start()
    gather_2(0)
    gather_end(1)
    products(1)
    pair_sums(2)
    gather_3(0)
    adapters(1)
    terms(1)
    core_copy(1).start()
    gather_end(0)
    products(0)
    pair_sums(1)
    suffix(2)
    adapters(0)
    terms(0)
    core_copy(0).start()
    suffix(1)
    pair_sums(0)
    finish(2)
    suffix(0)
    finish(1)
    for l in (2, 1, 0):
        adapters_end(l)
    finish(0)

    for l in range(LAYERS):
        out_copy(l).wait_recv()
        out_copy(l).wait_send()
        out_here(l).wait()
        pltpu.make_async_copy(la_v.at[l], la_hbm.at[l], out_sem.at[l]).wait()
        pltpu.make_async_copy(lb_v.at[l], lb_hbm.at[l], out_sem.at[LAYERS + l]).wait()
        core_copy(l).wait_send()
        for i in range(7):
            gather_out(l, i).wait_send()
        for j in range(1, TP):
            inner_copy(l, j, tp).wait_send()
            lora_b_copy(l, j, lax.rem(tp + j, TP), tp).wait_send()
        for j in range(1, CHIPS):
            to_owner(l, j, chip).wait_send()
            from_owner(l, j, chip).wait_send()
    for j in range(1, TP):
        squares_copy(j, tp).wait_send()


def per_device(
    queries, attention_output_grads, keys, hidden, value_weight, value_down_matrix, value_up_matrix,
    document_index, advantage, loss_token_mask, top_stream_gradient,
):
    hbm = pl.BlockSpec(memory_space=pl.ANY)
    vmem = pl.BlockSpec(memory_space=pltpu.VMEM)
    dma = pltpu.SemaphoreType.DMA
    scratch = [
        pltpu.VMEM((LAYERS, TOKENS, WIDTH), BF16),
        pltpu.VMEM((LAYERS, TOKENS, WIDTH), BF16),
        pltpu.VMEM((LAYERS, TOKENS, HEAD), BF16),
        pltpu.VMEM((LAYERS, TOKENS, WIDTH), BF16),
        pltpu.VMEM((LAYERS, WIDTH, WIDTH), BF16),
        pltpu.VMEM((LAYERS, WIDTH, RANK), BF16),
        pltpu.VMEM((LAYERS, RANK, WIDTH), BF16),
        pltpu.VMEM((ROWS, WIDTH), BF16),
        pltpu.VMEM((1152, 128), F32),
        pltpu.VMEM((TOKENS, 128), F32),
        pltpu.VMEM((TOKENS, 128), F32),
        pltpu.VMEM((LAYERS, TP, TOKENS, HEAD), BF16),
        pltpu.VMEM((LAYERS, TOKENS, RANK), F32),
        pltpu.VMEM((LAYERS, TOKENS, RANK), BF16),
        pltpu.VMEM((TOKENS, WIDTH), F32),
        pltpu.VMEM((LAYERS, TOKENS, 128), F32),
        pltpu.VMEM((8, TOKENS), F32),
        pltpu.VMEM((TP, 8, TOKENS), F32),
        pltpu.VMEM((LAYERS, 8, TOKENS), F32),
        pltpu.VMEM((LAYERS, TP, 8, TOKENS), F32),
        pltpu.VMEM((LAYERS, TP, RANK, HEAD), BF16),
        pltpu.VMEM((LAYERS, TP, RANK, HEAD), BF16),
        pltpu.VMEM((LAYERS, WIDTH, RANK), F32),
        pltpu.VMEM((LAYERS, RANK, HEAD), F32),
        pltpu.VMEM((LAYERS, TOKENS, WIDTH), BF16),
        pltpu.VMEM((LAYERS, HALF, WIDTH), BF16),
        pltpu.VMEM((LAYERS, HALF, WIDTH), BF16),
        pltpu.VMEM((LAYERS, CHIPS, ROWS, WIDTH), BF16),
        pltpu.VMEM((LAYERS, CHIPS, ROWS, WIDTH), BF16),
        pltpu.VMEM((LAYERS, HALF, WIDTH), BF16),
        pltpu.VMEM((ROWS, WIDTH), F32),
        pltpu.VMEM((LAYERS, HALF, WIDTH), BF16),
        pltpu.VMEM((LAYERS, HALF, WIDTH), BF16),
        dma((16,)), dma((3 * LAYERS,)),
        dma((LAYERS, 7)), dma((LAYERS, 7)), dma((7,)), dma((7,)), dma((LAYERS, 7)), dma((LAYERS, 7)),
        dma((LAYERS, 7)), dma((LAYERS, 7)),
        dma((LAYERS,)), dma((LAYERS,)), dma((LAYERS, 7)), dma((LAYERS, 7)), dma((LAYERS, 7)), dma((LAYERS, 7)),
        dma((LAYERS,)), dma((LAYERS,)),
    ]
    grad_in, lora_a, lora_b = pl.pallas_call(
        kernel,
        name="value_backward",
        out_shape=(
            jax.ShapeDtypeStruct((LAYERS, TOKENS, WIDTH), BF16),
            jax.ShapeDtypeStruct((LAYERS, WIDTH, RANK), F32),
            jax.ShapeDtypeStruct((LAYERS, RANK, HEAD), F32),
        ),
        in_specs=[hbm] * 8 + [vmem] * 3,
        out_specs=(hbm, hbm, hbm),
        scratch_shapes=scratch,
        compiler_params=pltpu.CompilerParams(
            collective_id=0, has_side_effects=True, vmem_limit_bytes=60 << 20
        ),
        cost_estimate=pl.CostEstimate(flops=8_000_000_000, bytes_accessed=22_000_000, transcendentals=4_000_000),
    )(
        queries[0], attention_output_grads[0], keys[0], hidden[0], value_weight[0], value_down_matrix[0],
        value_up_matrix[0], top_stream_gradient,
        document_index.reshape(1, TOKENS), advantage.reshape(1, TOKENS), loss_token_mask.reshape(1, TOKENS),
    )
    return grad_in[None], lora_a[None], lora_b[None]


def solution(mesh):
    in_specs = (
        P("pp", None, None, "tp"),
        P("pp", None, None, "tp"),
        P("pp", None, None, "tp"),
        P("pp", None, None, "tp"),
        P("pp", None, "tp", None),
        P("pp", None, "tp", None),
        P("pp", None, None, None),
        P(),
        P(),
        P(),
        P(None, "tp"),
    )
    out_specs = (P("pp", None, None, "tp"), P("pp", None, "tp", None), P("pp", None, None, "tp"))
    return jax.shard_map(
        per_device, mesh=mesh, in_specs=in_specs, out_specs=out_specs, check_vma=False
    )
```

time: 789 us -> 96.4 us (0.12)
  waiting for transfers between devices: 514 us -> 0 us
  other arithmetic: 148 us -> 0 us
  Pallas kernels: 0 us -> 86.1 us
  matrix products: 52.6 us -> 0 us
  blocking collectives: 32.9 us -> 0 us
  between operations: 14.5 us -> 0.64 us
  local copies, waits for them, and re-layouts: 19.2 us -> 9.43 us
    all_gather x4 -> x0, waiting for transfers between devices: 331 us -> none  [the longest x1 264 us: prefix(): gathered = lax.all_gather(x.astype(jnp.bfloat16), axis)]
    psum x2 -> x0, waiting for transfers between devices: 183 us -> none  [the longest x1 144 us: per_device(): lax.psum(stacked[1:].astype(jnp.bfloat16), 'pp').astype(jnp.float32)]
    add x14 -> x0, other arithmetic: 111 us -> none  [add_sums(): return earlier_sum + later_sum]
    pallas_call x0 -> x1, Pallas kernels: none -> 86.1 us  [per_device(): pl.pallas_call(kernel, name='value_backward', out_shape=(jax.ShapeDtypeSt...]
    dot_general x24 -> x0, matrix products: 52.6 us -> none  [the longest x3 13.7 us: one_block(): jnp.einsum('bgqh,kgh->gqbk', query_block, key_heads, preferred_element_ty...]
    psum x2 -> x0, blocking collectives: 32.9 us -> none  [the longest x1 18 us: per_device(): squares = lax.psum(jnp.sum(stream * stream, axis=1), 'tp')]
    another operation x5 -> x0, other arithmetic: 20.1 us -> none  [the longest x3 11.1 us: per_device(): stacked = jnp.stack(gradient_terms).astype(jnp.float32)]
  transfers between devices with their start and end apart: 6 -> 0, of which waited for: 5 -> 0; matrix products, arithmetic and copies ran while one was open for 8% -> 0% of each run, Pallas kernels for 0% -> 0%
where the time goes in v1:
time: 96.4 us; the launch traced here: 96.2 us
  Pallas kernels  86.1 us (89%)
  local copies, waits for them, and re-layouts  9.43 us (10%)
    pallas_call x1, Pallas kernels, per_device(): pl.pallas_call(kernel, name='value_backward', out_shape=(jax.ShapeDtypeSt...  86.1 us
    unnamed x6, local copies, waits for them, and re-layouts  9.43 us

profile of v1, /device:TPU:1, one launch (start us, length us, event | category | flops | bytes accessed | tf_op | source)
XLA Modules:
  0.0 96.2 jit_solution(11703537511400747915)
XLA Ops:
  0.6 2.2 %copy.14 = bf16[1,3,1024,64]{3,2,1,0:T(8,128)(2,1)} copy(bf16[1,3,1024,64]{2,3,1,0:T(8,128)(2,1)} %param.16) | data formatting | bytes 786432 | tf_op args[5]
  2.8 86.1 %value_backward.1 = (bf16[3,512,1024]{2,1,0:T(8,128)(2,1)}, f32[3,1024,64]{2,1,0:T(8,128)}, f32[3,64,128]{2,1,0:T(8,128)}) custom-call(bf16[3,512,1024]{2,1,0:T(8,128)(2,1)} %bitcast.18, bf16[3,512,1024]{2,1,0:T(8,128)(2,1)} %bitcast.19, bf16[3,512,128]{2,1,0:T(8,128)(2,1)} %bitcast.21, bf16[3,512,1024]{2,1,0:T(8,128)(2,1)} %bitcast.20, ...), custom_call_target="tpu_custom_call" | custom-call | flops 8000000000 | bytes 22000000 | tf_op jit(solution)/shard_map/value_backward/pallas_call | solution.py:464
  88.9 2.7 %copy.15 = f32[1,3,1024,64]{2,3,1,0:T(8,128)} copy(f32[1,3,1024,64]{3,2,1,0:T(8,128)} %bitcast.14) | data formatting | bytes 1572864
  91.6 0.0 copy-start
  91.6 3.9 %copy.18 = bf16[1,3,512,1024]{3,2,1,0:T(8,128)(2,1)} copy(bf16[1,3,512,1024]{3,2,1,0:T(8,128)(2,1)} %bitcast.13) | data formatting | bytes 6291456
  95.5 0.0 copy-done
  95.5 0.6 copy.19
Async XLA Ops:
  91.6 3.9 %copy-start = (f32[3,64,128]{2,1,0:T(8,128)S(1)}, f32[3,64,128]{2,1,0:T(8,128)}, u32[]{:S(2)}) copy-start(f32[3,64,128]{2,1,0:T(8,128)} %get-tuple-element.8) | copy-start | bytes 294916

commit v2 on v1

v2 whole, which is shorter than its diff:
```python
import jax
import jax.numpy as jnp
from jax import lax
from jax.experimental import pallas as pl
from jax.experimental.pallas import tpu as pltpu
from jax.sharding import PartitionSpec as P

MESH = pl.DeviceIdType.MESH
BF16 = jnp.bfloat16
F32 = jnp.float32
LAYERS = 3
TOKENS = 512
WIDTH = 1024
HEAD = 128
HEADS = 8
RANK = 64
SPAN = 256
HALF = 128
ROWS = 16
CHIPS = 8
TP = 8
MODEL = 8192
SEGS = 8
LOG2E = 1.4426950408889634
CHUNKS = ((1, 0, 2), (2, 0, 2), (0, 0, 2))
SOFTMAX_SCALE = HEAD**-0.5 * LOG2E
MASK_OFFSET = (0, 128, 384, 768)


def dot(a, b, dims):
    return lax.dot_general(a, b, (dims, ((), ())), preferred_element_type=F32)


def kernel(
    q_hbm, g_hbm, k_hbm, h_hbm, w_hbm, dn_hbm, up_hbm, top_hbm, doc_ref, adv_ref, loss_ref,
    out_hbm, la_hbm, lb_hbm,
    q_v, g_v, k_v, h_v, w_v, dn_v, up_v, top_v,
    mask_v, weight_v, acc_v, vg_v, hd_v, ad_v, ng_v, inv_v,
    sqs_v, sqr_v, ins_v, inr_v, lbs_v, lbr_v, la_v, lb_v,
    t_v, tp_v, p_v, q8_v, rs_v, rr_v, carry_v, own_v, peer_v,
    in_sem, out_sem,
    gs_sem, gr_sem, sqs_sem, sqr_sem, ins_sem, inr_sem, lbs_sem, lbr_sem,
    cs_sem, cr_sem, p1s_sem, p1r_sem, p2s_sem, p2r_sem, os_sem, or_sem,
):
    pp = lax.axis_index("pp")
    tp = lax.axis_index("tp")
    core = lax.rem(pp, 2)
    chip = lax.div(pp, 2)
    yl = lax.div(tp, 4)
    x = lax.rem(tp, 4)

    yl_peer = (pp, (1 - yl) * 4 + x)
    x_up = (pp, yl * 4 + lax.rem(x + 1, 4))
    x_down = (pp, yl * 4 + lax.rem(x + 3, 4))
    core_peer = (chip * 2 + (1 - core), tp)

    def tp_peer(j):
        return (pp, lax.rem(tp + j, TP))

    def chip_index(j):
        return lax.rem(chip + j, CHIPS)

    def chip_peer(j):
        return (chip_index(j) * 2 + core, tp)

    copies = {}

    def load(name, src, dst):
        copies[name] = pltpu.make_async_copy(src, dst, in_sem.at[len(copies)])

    for l in (2, 1, 0):
        load(("k", l), k_hbm.at[l], k_v.at[l])
        load(("q", l), q_hbm.at[l], q_v.at[l])
        load(("g", l), g_hbm.at[l], g_v.at[l])
    load("h", h_hbm, h_v)
    load("dn", dn_hbm, dn_v)
    load("up", up_hbm, up_v)
    for l in (2, 1, 0):
        load(("w", l), w_hbm.at[l], w_v.at[l])
    load("top", top_hbm.at[:, core, chip], top_v)
    first = [(name, LAYERS - 1) for name in "kqg"]
    for name in first:
        copies[name].start()

    barrier = pltpu.get_barrier_semaphore()
    for j in range(1, TP):
        pl.semaphore_signal(barrier, inc=1, device_id=tp_peer(j), device_id_type=MESH)
    for j in range(1, CHIPS):
        pl.semaphore_signal(barrier, inc=1, device_id=chip_peer(j), device_id_type=MESH)
    pl.semaphore_signal(barrier, inc=1, device_id=core_peer, device_id_type=MESH)

    def remote(src, dst, send, recv, device):
        return pltpu.make_async_remote_copy(
            src_ref=src, dst_ref=dst, send_sem=send, recv_sem=recv, device_id=device, device_id_type=MESH
        )

    def columns(row):
        return jnp.transpose(jnp.broadcast_to(row, (128, TOKENS)))

    def rows_of(sums):
        parts = [sums[128 * i : 128 * i + 128, :] for i in range(sums.shape[0] // 128)]
        return jnp.concatenate([jnp.sum(jnp.transpose(part), axis=0, keepdims=True) for part in parts], axis=0)

    def columns_of(rows):
        return jnp.concatenate(
            [jnp.transpose(jnp.broadcast_to(rows[i : i + 1, :], (128, 128))) for i in range(rows.shape[0])], axis=0
        )

    doc_row = doc_ref[...].astype(F32)
    doc_col = columns(doc_row)
    key_pos = lax.broadcasted_iota(jnp.int32, (128, 128), 0)
    query_pos = lax.broadcasted_iota(jnp.int32, (128, 128), 1)
    for b in range(4):
        low = max(0, b - 2)
        for kb in range(low, b + 1):
            allowed = doc_col[128 * kb : 128 * kb + 128, :] == doc_row[:, 128 * b : 128 * b + 128]
            if kb == b:
                allowed = allowed & (key_pos <= query_pos)
            at = MASK_OFFSET[b] + 128 * (kb - low)
            mask_v[at : at + 128, :] = jnp.where(allowed, 0.0, -jnp.inf)
    loss_row = loss_ref[...].astype(F32)
    labels = lax.broadcasted_iota(jnp.int32, (SEGS, TOKENS), 0).astype(F32)
    member = jnp.where(labels == doc_row, 1.0, 0.0)
    counts = jnp.sum(member * loss_row, axis=1, keepdims=True)
    per_token = jnp.sum(member * (1.0 / jnp.maximum(counts, 1.0)), axis=0, keepdims=True)
    weights = columns(adv_ref[...].astype(F32) * loss_row * per_token * (TOKENS / SEGS))
    weight_v[...] = weights.reshape(2, 2, CHIPS, ROWS, 128)

    slot = x * 2 + yl
    other = x * 2 + (1 - yl)
    left = lax.rem(x + 3, 4) * 2
    right = lax.rem(x + 1, 4) * 2
    across = lax.rem(x + 2, 4) * 2

    def attention(l):
        for name in ("k", "q", "g"):
            copies[(name, l)].wait()
        if l == LAYERS - 1:
            for name in copies:
                if name not in first:
                    copies[name].start()
        for b in range(4):
            low, high = max(0, b - 2) * 128, (b + 1) * 128
            keys = k_v[l, low:high, :]
            mask = mask_v[MASK_OFFSET[b] : MASK_OFFSET[b] + high - low, :]
            mask4 = jnp.concatenate([mask] * 4, axis=1)
            total = None
            for part in range(2):
                heads = range(4 * part, 4 * part + 4)
                block = slice(128 * b, 128 * b + 128)
                queries = jnp.concatenate([q_v[l, block, HEAD * i : HEAD * i + HEAD] for i in heads], axis=0)
                grads = jnp.concatenate([g_v[l, block, HEAD * i : HEAD * i + HEAD] for i in heads], axis=0)
                scores = dot(keys, queries, ((1,), (1,))) + mask4
                peak = jnp.max(scores, axis=0, keepdims=True)
                expo = jnp.exp2((scores - peak) * SOFTMAX_SCALE)
                probs = (expo * (1.0 / jnp.sum(expo, axis=0, keepdims=True))).astype(BF16)
                piece = dot(probs, grads, ((1,), (0,)))
                total = piece if total is None else total + piece
            if b == 0:
                acc_v[0:128, :] = total
            else:
                acc_v[low : high - 128, :] += total[: high - low - 128]
                acc_v[high - 128 : high, :] = total[high - low - 128 :]
        vg_v[l, slot] = acc_v[...].astype(BF16)

    def spans(chunk):
        return pl.ds(chunk[1], chunk[2])

    def tokens(chunk):
        return slice(chunk[1] * SPAN, (chunk[1] + chunk[2]) * SPAN)

    def index(chunk):
        return chunk[0] * 2 + chunk[1]

    def gather_copy(chunk, i, place, device):
        part = vg_v.at[chunk[0], place, pl.ds(chunk[1] * SPAN, chunk[2] * SPAN)]
        return remote(part, part, gs_sem.at[index(chunk), i], gr_sem.at[index(chunk), i], device)

    def gather_out(chunk, i):
        return (
            lambda: gather_copy(chunk, 0, slot, yl_peer),
            lambda: gather_copy(chunk, 1, slot, x_up),
            lambda: gather_copy(chunk, 2, slot, x_down),
            lambda: gather_copy(chunk, 3, other, x_up),
            lambda: gather_copy(chunk, 4, other, x_down),
            lambda: gather_copy(chunk, 5, left + yl, x_up),
            lambda: gather_copy(chunk, 6, right + (1 - yl), x_down),
        )[i]()

    def gather_in(chunk, i):
        place = (other, left + yl, right + yl, left + (1 - yl), right + (1 - yl), across + yl, across + (1 - yl))[i]
        return gather_copy(chunk, i, place, yl_peer)

    def gather_1(chunk):
        for i in (0, 1, 2):
            gather_out(chunk, i).start()

    def gather_2(chunk):
        gather_in(chunk, 0).wait_recv()
        for i in (3, 4):
            gather_out(chunk, i).start()

    def gather_3(chunk):
        gather_in(chunk, 1).wait_recv()
        gather_out(chunk, 5).start()

    def gather_4(chunk):
        gather_in(chunk, 4).wait_recv()
        gather_out(chunk, 6).start()

    def gather_end(chunk):
        for i in (2, 3, 5, 6):
            gather_in(chunk, i).wait_recv()

    def squares_and_low():
        sqs_v[...] = jnp.zeros((16, 128), F32)
        copies["h"].wait()
        copies["dn"].wait()
        for l in range(LAYERS):
            sums = None
            for n in range(WIDTH // 128):
                part = h_v[l, :, 128 * n : 128 * n + 128].astype(F32)
                sums = part * part if sums is None else sums + part * part
            sqs_v[4 * l : 4 * l + 4, :] = rows_of(sums)
            hd_v[l] = dot(h_v[l], dn_v[l], ((1,), (1,)))
        sqr_v[tp] = sqs_v[...]

    def squares_copy(j, place):
        return remote(sqs_v, sqr_v.at[place], sqs_sem.at[j - 1], sqr_sem.at[j - 1], tp_peer(j))

    def squares_send():
        for j in range(1, TP):
            squares_copy(j, tp).start()

    def squares_wait():
        for j in range(1, TP):
            squares_copy(j, lax.rem(tp - j + TP, TP)).wait_recv()
        total = sqr_v[0]
        for i in range(1, TP):
            total = total + sqr_v[i]
        inverse = lax.rsqrt(total * (1.0 / MODEL) + 1e-5)
        for l in range(LAYERS):
            inv_v[l] = columns_of(inverse[4 * l : 4 * l + 4, :])

    def gathered(l, rows):
        return jnp.concatenate([vg_v[l, (j % 4) * 2 + j // 4, rows] for j in range(TP)], axis=1)

    def inner_copy(chunk, j, place):
        at = index(chunk)
        return remote(ins_v.at[at], inr_v.at[at, place], ins_sem.at[at, j - 1], inr_sem.at[at, j - 1], tp_peer(j))

    def products(chunk):
        l, at, rows = chunk[0], index(chunk), tokens(chunk)
        if l == LAYERS - 1 and chunk[1] == 0:
            copies["up"].wait()
        if chunk[1] == 0:
            copies[("w", l)].wait()
        ad_v[l, rows] = dot(gathered(l, rows), up_v[l], ((1,), (1,))).astype(BF16)
        acc_v[rows] = jnp.zeros((chunk[2] * SPAN, 128), F32)

        def one(n, unused):
            cols = pl.ds(pl.multiple_of(n * 256, 256), 256)
            twice = (ad_v[l, rows].astype(F32) * 2.0).astype(BF16)
            ng = dot(gathered(l, rows), w_v[l, cols, :], ((1,), (1,))) + dot(twice, dn_v[l, :, cols], ((1,), (0,)))
            ng_v[l % 2, rows, cols] = ng
            prod = h_v[l, rows, cols].astype(F32) * ng
            acc_v[rows] += prod[:, :128] + prod[:, 128:]
            return unused

        lax.fori_loop(0, WIDTH // 256, one, 0)
        row = rows_of(acc_v[rows])
        ins_v[at] = jnp.concatenate([row] * (4 // chunk[2]), axis=0)
        inr_v[at, tp] = ins_v[at]
        for j in range(1, TP):
            inner_copy(chunk, j, tp).start()

    def terms(chunk):
        l, at, rows = chunk[0], index(chunk), tokens(chunk)
        for j in range(1, TP):
            inner_copy(chunk, j, lax.rem(tp - j + TP, TP)).wait_recv()
        total = inr_v[at, 0]
        for i in range(1, TP):
            total = total + inr_v[at, i]
        inv = inv_v[l, rows]
        acc_v[rows] = inv * inv * inv * columns_of(total[0 : 2 * chunk[2], :]) * (1.0 / MODEL)

        def one(n, unused):
            cols = pl.ds(pl.multiple_of(n * 128, 128), 128)
            term = inv_v[l, rows] * ng_v[l % 2, rows, cols] - acc_v[rows] * h_v[l, rows, cols].astype(F32)
            t_v[l, spans(chunk), :, :, cols] = term.astype(BF16).reshape(chunk[2], 2, HALF, 128)
            return unused

        lax.fori_loop(0, WIDTH // 128, one, 0)

    def lora_b_copy(l, j, block, place):
        return remote(lbs_v.at[l, block], lbr_v.at[l, place], lbs_sem.at[l, j - 1], lbr_sem.at[l, j - 1], tp_peer(j))

    def adapters(l):
        inv = inv_v[l][:, :RANK]
        scaled = (2.0 * inv * ad_v[l].astype(F32)).astype(BF16)
        la_v[l] = dot(scaled, h_v[l], ((0,), (0,)))
        low = (2.0 * inv * hd_v[l]).astype(BF16)
        part = dot(low, gathered(l, slice(0, TOKENS)), ((0,), (0,)))
        for j in range(TP):
            lbs_v[l, j] = part[:, 128 * j : 128 * j + 128].astype(BF16)
        lbr_v[l, tp] = lbs_v[l, tp]
        for j in range(1, TP):
            lora_b_copy(l, j, lax.rem(tp + j, TP), tp).start()
        pltpu.make_async_copy(la_v.at[l], la_hbm.at[l], out_sem.at[l]).start()

    def adapters_end(l):
        for j in range(1, TP):
            lora_b_copy(l, j, 0, lax.rem(tp - j + TP, TP)).wait_recv()
        total = lbr_v[l, 0].astype(F32)
        for i in range(1, TP):
            total = total + lbr_v[l, i].astype(F32)
        lb_v[l] = total
        pltpu.make_async_copy(lb_v.at[l], lb_hbm.at[l], out_sem.at[LAYERS + l]).start()

    def core_copy(chunk):
        at = index(chunk)
        return remote(
            t_v.at[chunk[0], spans(chunk), 1 - core], tp_v.at[chunk[0], spans(chunk)],
            cs_sem.at[at], cr_sem.at[at], core_peer,
        )

    def to_owner(chunk, j, place):
        at = index(chunk)
        return remote(
            p_v.at[chunk[0], spans(chunk), chip_index(j)], q8_v.at[chunk[0], place, spans(chunk)],
            p1s_sem.at[at, j - 1], p1r_sem.at[at, j - 1], chip_peer(j),
        )

    def from_owner(chunk, j, place):
        at = index(chunk)
        return remote(
            rs_v.at[chunk[0], chip_index(j), spans(chunk)], rr_v.at[chunk[0], spans(chunk), place],
            p2s_sem.at[at, j - 1], p2r_sem.at[at, j - 1], chip_peer(j),
        )

    def source(j):
        return lax.rem(chip - j + CHIPS, CHIPS)

    def pair_sums(chunk):
        l, ts = chunk[0], spans(chunk)
        core_copy(chunk).wait_recv()
        both = t_v[l, ts, core].astype(F32) + tp_v[l, ts].astype(F32)
        p_v[l, ts] = both.reshape(chunk[2], CHIPS, ROWS, WIDTH).astype(BF16)
        for j in (4, 2, 6, 1, 3, 5, 7):
            to_owner(chunk, j, chip).start()
        q8_v[l, chip, ts] = p_v[l, ts, chip]

    def suffix(chunk):
        l, ts = chunk[0], spans(chunk)
        if l == LAYERS - 1:
            if chunk[1] == 0:
                copies["top"].wait()
            weights = jnp.concatenate([weight_v[ts, core, chip]] * (WIDTH // 128), axis=2)
            carry = weights * top_v[ts].astype(F32)
        else:
            carry = carry_v[ts]
        for j in range(1, CHIPS):
            to_owner(chunk, j, source(j)).wait_recv()
        for i in reversed(range(CHIPS)):
            rs_v[l, i, ts] = carry.astype(BF16)
            carry = carry + q8_v[l, i, ts].astype(F32)
        carry_v[ts] = carry
        for j in (4, 2, 6, 1, 3, 5, 7):
            from_owner(chunk, j, chip).start()
        rr_v[l, ts, chip] = rs_v[l, chip, ts]

    def out_copy(chunk):
        at = index(chunk)
        return remote(
            peer_v.at[chunk[0], spans(chunk)], out_hbm.at[chunk[0], spans(chunk), core],
            os_sem.at[at], or_sem.at[at], core_peer,
        )

    def out_in(chunk):
        at = index(chunk)
        return remote(
            peer_v.at[chunk[0], spans(chunk)], out_hbm.at[chunk[0], spans(chunk), 1 - core],
            os_sem.at[at], or_sem.at[at], core_peer,
        )

    def out_here(chunk):
        return pltpu.make_async_copy(
            own_v.at[chunk[0], spans(chunk)], out_hbm.at[chunk[0], spans(chunk), core], out_sem.at[2 * LAYERS + index(chunk)]
        )

    def finish(chunk):
        l, ts = chunk[0], spans(chunk)
        for j in range(1, CHIPS):
            from_owner(chunk, j, source(j)).wait_recv()
        first = (1 - core).astype(F32)
        second = core.astype(F32)
        carry = rr_v[l, ts].astype(F32).reshape(chunk[2], HALF, WIDTH)
        term = t_v[l, ts, core].astype(F32)
        peer_term = tp_v[l, ts].astype(F32)
        peer_v[l, ts] = (carry + peer_term + second * term).astype(BF16)
        out_copy(chunk).start()
        own_v[l, ts] = (carry + term + first * peer_term).astype(BF16)
        out_here(chunk).start()

    attention(2)
    pl.semaphore_wait(barrier, TP + CHIPS - 1)
    gather_1((2, 0, 2))
    attention(1)
    gather_1((1, 0, 2))
    gather_2((2, 0, 2))
    gather_3((2, 0, 2))
    squares_and_low()
    squares_send()
    gather_2((1, 0, 2))
    gather_4((2, 0, 2))
    attention(0)
    gather_4((1, 0, 2))
    gather_3((1, 0, 2))
    gather_1((0, 0, 2))
    gather_end((2, 0, 2))
    products((2, 0, 2))
    gather_2((0, 0, 2))
    gather_end((1, 0, 2))
    products((1, 0, 2))
    squares_wait()
    terms((2, 0, 2))
    core_copy((2, 0, 2)).start()
    gather_4((0, 0, 2))
    gather_3((0, 0, 2))
    adapters(1)
    pair_sums((2, 0, 2))
    terms((1, 0, 2))
    core_copy((1, 0, 2)).start()
    gather_end((0, 0, 2))
    pair_sums((1, 0, 2))
    products((0, 0, 2))
    suffix((2, 0, 2))
    terms((0, 0, 2))
    adapters(2)
    core_copy((0, 0, 2)).start()
    pair_sums((0, 0, 2))
    suffix((1, 0, 2))
    suffix((0, 0, 2))
    adapters_end(2)
    finish((1, 0, 2))
    adapters(0)
    adapters_end(1)
    finish((2, 0, 2))
    finish((0, 0, 2))
    adapters_end(0)

    for chunk in CHUNKS:
        out_in(chunk).wait_recv()
        out_copy(chunk).wait_send()
        out_here(chunk).wait()
        core_copy(chunk).wait_send()
        for i in range(7):
            gather_out(chunk, i).wait_send()
        for j in range(1, TP):
            inner_copy(chunk, j, tp).wait_send()
        for j in range(1, CHIPS):
            to_owner(chunk, j, chip).wait_send()
            from_owner(chunk, j, chip).wait_send()
    for l in range(LAYERS):
        pltpu.make_async_copy(la_v.at[l], la_hbm.at[l], out_sem.at[l]).wait()
        pltpu.make_async_copy(lb_v.at[l], lb_hbm.at[l], out_sem.at[LAYERS + l]).wait()
        for j in range(1, TP):
            lora_b_copy(l, j, lax.rem(tp + j, TP), tp).wait_send()
    for j in range(1, TP):
        squares_copy(j, tp).wait_send()


def place(grad_ref, a_ref, b_ref, grad_out, a_out, b_out, grad_v, a_v, b_v, in_sem, out_sem):
    pieces = [(a_ref, a_v, a_out), (b_ref, b_v, b_out)]
    for l in range(LAYERS):
        for t in range(2):
            at = (l, t)
            pieces.append((grad_ref.at[at], grad_v.at[at], grad_out.at[at]))
    reads = [pltpu.make_async_copy(src, mid, in_sem.at[i]) for i, (src, mid, _) in enumerate(pieces)]
    writes = [pltpu.make_async_copy(mid, dst, out_sem.at[i]) for i, (_, mid, dst) in enumerate(pieces)]
    for copy in reads:
        copy.start()
    for read, write in zip(reads, writes):
        read.wait()
        write.start()
    for copy in writes:
        copy.wait()


def per_device(
    queries, attention_output_grads, keys, hidden, value_weight, value_down_matrix, value_up_matrix,
    document_index, advantage, loss_token_mask, top_stream_gradient,
):
    hbm = pl.BlockSpec(memory_space=pl.ANY)
    vmem = pl.BlockSpec(memory_space=pltpu.VMEM)
    dma = pltpu.SemaphoreType.DMA
    scratch = [
        pltpu.VMEM((LAYERS, TOKENS, WIDTH), BF16),
        pltpu.VMEM((LAYERS, TOKENS, WIDTH), BF16),
        pltpu.VMEM((LAYERS, TOKENS, HEAD), BF16),
        pltpu.VMEM((LAYERS, TOKENS, WIDTH), BF16),
        pltpu.VMEM((LAYERS, WIDTH, WIDTH), BF16),
        pltpu.VMEM((LAYERS, RANK, WIDTH), BF16),
        pltpu.VMEM((LAYERS, RANK, WIDTH), BF16),
        pltpu.VMEM((2, ROWS, WIDTH), BF16),
        pltpu.VMEM((1152, 128), F32),
        pltpu.VMEM((2, 2, CHIPS, ROWS, 128), F32),
        pltpu.VMEM((TOKENS, 128), F32),
        pltpu.VMEM((LAYERS, TP, TOKENS, HEAD), BF16),
        pltpu.VMEM((LAYERS, TOKENS, RANK), F32),
        pltpu.VMEM((LAYERS, TOKENS, RANK), BF16),
        pltpu.VMEM((2, TOKENS, WIDTH), F32),
        pltpu.VMEM((LAYERS, TOKENS, 128), F32),
        pltpu.VMEM((16, 128), F32),
        pltpu.VMEM((TP, 16, 128), F32),
        pltpu.VMEM((2 * LAYERS, 8, 128), F32),
        pltpu.VMEM((2 * LAYERS, TP, 8, 128), F32),
        pltpu.VMEM((LAYERS, TP, RANK, HEAD), BF16),
        pltpu.VMEM((LAYERS, TP, RANK, HEAD), BF16),
        pltpu.VMEM((LAYERS, RANK, WIDTH), F32),
        pltpu.VMEM((LAYERS, RANK, HEAD), F32),
        pltpu.VMEM((LAYERS, 2, 2, HALF, WIDTH), BF16),
        pltpu.VMEM((LAYERS, 2, HALF, WIDTH), BF16),
        pltpu.VMEM((LAYERS, 2, CHIPS, ROWS, WIDTH), BF16),
        pltpu.VMEM((LAYERS, CHIPS, 2, ROWS, WIDTH), BF16),
        pltpu.VMEM((LAYERS, CHIPS, 2, ROWS, WIDTH), BF16),
        pltpu.VMEM((LAYERS, 2, CHIPS, ROWS, WIDTH), BF16),
        pltpu.VMEM((2, ROWS, WIDTH), F32),
        pltpu.VMEM((LAYERS, 2, HALF, WIDTH), BF16),
        pltpu.VMEM((LAYERS, 2, HALF, WIDTH), BF16),
        dma((16,)), dma((4 * LAYERS,)),
        dma((2 * LAYERS, 7)), dma((2 * LAYERS, 7)), dma((7,)), dma((7,)), dma((2 * LAYERS, 7)), dma((2 * LAYERS, 7)),
        dma((LAYERS, 7)), dma((LAYERS, 7)),
        dma((2 * LAYERS,)), dma((2 * LAYERS,)),
        dma((2 * LAYERS, 7)), dma((2 * LAYERS, 7)), dma((2 * LAYERS, 7)), dma((2 * LAYERS, 7)),
        dma((2 * LAYERS,)), dma((2 * LAYERS,)),
    ]
    grad_in, lora_a, lora_b = pl.pallas_call(
        kernel,
        name="value_backward",
        out_shape=(
            jax.ShapeDtypeStruct((LAYERS, 2, 2, HALF, WIDTH), BF16),
            jax.ShapeDtypeStruct((LAYERS, RANK, WIDTH), F32),
            jax.ShapeDtypeStruct((LAYERS, RANK, HEAD), F32),
        ),
        in_specs=[hbm] * 8 + [vmem] * 3,
        out_specs=(hbm, hbm, hbm),
        scratch_shapes=scratch,
        compiler_params=pltpu.CompilerParams(
            collective_id=0, has_side_effects=True, vmem_limit_bytes=60 << 20
        ),
        cost_estimate=pl.CostEstimate(flops=8_000_000_000, bytes_accessed=22_000_000, transcendentals=4_000_000),
    )(
        queries[0], attention_output_grads[0], keys[0], hidden[0], value_weight[0], jnp.swapaxes(value_down_matrix[0], 1, 2),
        value_up_matrix[0], top_stream_gradient.reshape(2, 2, CHIPS, ROWS, WIDTH),
        document_index.reshape(1, TOKENS), advantage.reshape(1, TOKENS), loss_token_mask.reshape(1, TOKENS),
    )
    grad_in, lora_a, lora_b = pl.pallas_call(
        place,
        name="place",
        out_shape=(
            jax.ShapeDtypeStruct(grad_in.shape, BF16),
            jax.ShapeDtypeStruct(lora_a.shape, F32),
            jax.ShapeDtypeStruct(lora_b.shape, F32),
        ),
        in_specs=[hbm] * 3,
        out_specs=(hbm, hbm, hbm),
        scratch_shapes=[
            pltpu.VMEM(grad_in.shape, BF16),
            pltpu.VMEM(lora_a.shape, F32),
            pltpu.VMEM(lora_b.shape, F32),
            dma((8,)), dma((8,)),
        ],
        compiler_params=pltpu.CompilerParams(vmem_limit_bytes=60 << 20),
    )(grad_in, lora_a, lora_b)
    return grad_in.reshape(1, LAYERS, TOKENS, WIDTH), jnp.swapaxes(lora_a, 1, 2)[None], lora_b[None]


def solution(mesh):
    in_specs = (
        P("pp", None, None, "tp"),
        P("pp", None, None, "tp"),
        P("pp", None, None, "tp"),
        P("pp", None, None, "tp"),
        P("pp", None, "tp", None),
        P("pp", None, "tp", None),
        P("pp", None, None, None),
        P(),
        P(),
        P(),
        P(None, "tp"),
    )
    out_specs = (P("pp", None, None, "tp"), P("pp", None, "tp", None), P("pp", None, None, "tp"))
    return jax.shard_map(
        per_device, mesh=mesh, in_specs=in_specs, out_specs=out_specs, check_vma=False
    )
```

time: 96.4 us -> 86.9 us (0.901)
  local copies, waits for them, and re-layouts: 9.43 us -> 0 us
    unnamed x6 -> x0, local copies, waits for them, and re-layouts: 9.43 us -> none
    pallas_call x1, Pallas kernels: 86.1 us -> 82.7 us  [per_device(): pl.pallas_call(kernel, name='value_backward', out_shape=(jax.ShapeDtypeSt...]
    pallas_call x0 -> x1, Pallas kernels: none -> 3.22 us  [per_device(): pl.pallas_call(place, name='place', out_shape=(jax.ShapeDtypeStruct(grad_...]
where the time goes in v2:
time: 86.9 us; the launch traced here: 86.7 us
  Pallas kernels  85.9 us (99%)
    pallas_call x1, Pallas kernels, per_device(): pl.pallas_call(kernel, name='value_backward', out_shape=(jax.ShapeDtypeSt...  82.7 us
    pallas_call x1, Pallas kernels, per_device(): pl.pallas_call(place, name='place', out_shape=(jax.ShapeDtypeStruct(grad_...  3.22 us

profile of v2, /device:TPU:1, one launch (start us, length us, event | category | flops | bytes accessed | tf_op | source)
XLA Modules:
  0.0 86.7 jit_solution(3335637700073065502)
XLA Ops:
  0.6 82.7 %value_backward.1 = (bf16[3,2,2,128,1024]{4,3,2,1,0:T(8,128)(2,1)}, f32[3,64,1024]{2,1,0:T(8,128)}, f32[3,64,128]{2,1,0:T(8,128)}) custom-call(bf16[3,512,1024]{2,1,0:T(8,128)(2,1)} %bitcast.19, bf16[3,512,1024]{2,1,0:T(8,128)(2,1)} %bitcast.20, bf16[3,512,128]{2,1,0:T(8,128)(2,1)} %bitcast.25, bf16[3,512,1024]{2,1,0:T(8,128)(2,1)} %bitcast.21, ...), custom_call_target="tpu_custom_call" | custom-call | flops 8000000000 | bytes 22000000 | tf_op jit(solution)/shard_map/value_backward/pallas_call | solution.py:538
  83.3 3.2 %place.1 = (bf16[3,2,2,128,1024]{4,3,2,1,0:T(8,128)(2,1)}, f32[3,64,1024]{2,1,0:T(8,128)}, f32[3,64,128]{2,1,0:T(8,128)}) custom-call(bf16[3,2,2,128,1024]{4,3,2,1,0:T(8,128)(2,1)} %get-tuple-element.9.grad_ref, f32[3,64,1024]{2,1,0:T(8,128)} %get-tuple-element.10.a_ref, f32[3,64,128]{2,1,0:T(8,128)} %get-tuple-element.11.b_ref), custom_call_target="tpu_custom_call" | custom-call | tf_op jit(solution)/shard_map/place/pallas_call | solution.py:558

commit v3 on v2

--- a/solution.py
+++ b/solution.py
@@ -16,13 +16,15 @@
 RANK = 64
 SPAN = 256
 HALF = 128
-ROWS = 16
-CHIPS = 8
+ROWS = 32
+CHIPS = 4
 TP = 8
 MODEL = 8192
 SEGS = 8
 LOG2E = 1.4426950408889634
-CHUNKS = ((1, 0, 2), (2, 0, 2), (0, 0, 2))
+GATHER_CHUNKS = ((2, 1, 1), (2, 0, 1), (1, 0, 2), (0, 0, 2))
+PRODUCT_CHUNKS = ((2, 0, 1), (2, 1, 1), (1, 0, 2), (0, 0, 2))
+SUM_CHUNKS = ((2, 0, 1), (0, 0, 1), (2, 1, 1), (1, 0, 2), (0, 1, 1))
 SOFTMAX_SCALE = HEAD**-0.5 * LOG2E
 MASK_OFFSET = (0, 128, 384, 768)
 
@@ -37,22 +39,24 @@
     q_v, g_v, k_v, h_v, w_v, dn_v, up_v, top_v,
     mask_v, weight_v, acc_v, vg_v, hd_v, ad_v, ng_v, inv_v,
     sqs_v, sqr_v, ins_v, inr_v, lbs_v, lbr_v, la_v, lb_v,
-    t_v, tp_v, p_v, q8_v, rs_v, rr_v, carry_v, own_v, peer_v,
+    t_v, tp_v, p_v, q8_v, rs_v, rr_v, carry_v, tots_v, totr_v, own_v, peer_v,
     in_sem, out_sem,
     gs_sem, gr_sem, sqs_sem, sqr_sem, ins_sem, inr_sem, lbs_sem, lbr_sem,
-    cs_sem, cr_sem, p1s_sem, p1r_sem, p2s_sem, p2r_sem, os_sem, or_sem,
+    cs_sem, cr_sem, p1s_sem, p1r_sem, p2s_sem, p2r_sem, hs_sem, hr_sem, os_sem, or_sem,
 ):
     pp = lax.axis_index("pp")
     tp = lax.axis_index("tp")
     core = lax.rem(pp, 2)
-    chip = lax.div(pp, 2)
+    chip = lax.rem(lax.div(pp, 2), CHIPS)
+    half = lax.div(pp, 2 * CHIPS)
     yl = lax.div(tp, 4)
     x = lax.rem(tp, 4)
 
     yl_peer = (pp, (1 - yl) * 4 + x)
     x_up = (pp, yl * 4 + lax.rem(x + 1, 4))
     x_down = (pp, yl * 4 + lax.rem(x + 3, 4))
-    core_peer = (chip * 2 + (1 - core), tp)
+    core_peer = (pp + 1 - 2 * core, tp)
+    half_peer = (lax.rem(pp + 2 * CHIPS, 4 * CHIPS), tp)
 
     def tp_peer(j):
         return (pp, lax.rem(tp + j, TP))
@@ -61,7 +65,7 @@
         return lax.rem(chip + j, CHIPS)
 
     def chip_peer(j):
-        return (chip_index(j) * 2 + core, tp)
+        return ((half * CHIPS + chip_index(j)) * 2 + core, tp)
 
     copies = {}
 
@@ -87,7 +91,8 @@
         pl.semaphore_signal(barrier, inc=1, device_id=tp_peer(j), device_id_type=MESH)
     for j in range(1, CHIPS):
         pl.semaphore_signal(barrier, inc=1, device_id=chip_peer(j), device_id_type=MESH)
-    pl.semaphore_signal(barrier, inc=1, device_id=core_peer, device_id_type=MESH)
+    for peer in (core_peer, half_peer):
+        pl.semaphore_signal(barrier, inc=1, device_id=peer, device_id_type=MESH)
 
     def remote(src, dst, send, recv, device):
         return pltpu.make_async_remote_copy(
@@ -346,9 +351,26 @@
         core_copy(chunk).wait_recv()
         both = t_v[l, ts, core].astype(F32) + tp_v[l, ts].astype(F32)
         p_v[l, ts] = both.reshape(chunk[2], CHIPS, ROWS, WIDTH).astype(BF16)
-        for j in (4, 2, 6, 1, 3, 5, 7):
+        for j in (2, 1, 3):
             to_owner(chunk, j, chip).start()
         q8_v[l, chip, ts] = p_v[l, ts, chip]
+
+    def total_copy(chunk):
+        at = index(chunk)
+        return remote(
+            tots_v.at[chunk[0], spans(chunk)], totr_v.at[chunk[0], spans(chunk)],
+            hs_sem.at[at], hr_sem.at[at], half_peer,
+        )
+
+    def totals(chunk):
+        l, ts = chunk[0], spans(chunk)
+        for j in range(1, CHIPS):
+            to_owner(chunk, j, source(j)).wait_recv()
+        total = q8_v[l, 0, ts].astype(F32)
+        for i in range(1, CHIPS):
+            total = total + q8_v[l, i, ts].astype(F32)
+        tots_v[l, ts] = total.astype(BF16)
+        total_copy(chunk).start()
 
     def suffix(chunk):
         l, ts = chunk[0], spans(chunk)
@@ -359,13 +381,14 @@
             carry = weights * top_v[ts].astype(F32)
         else:
             carry = carry_v[ts]
-        for j in range(1, CHIPS):
-            to_owner(chunk, j, source(j)).wait_recv()
+        total_copy(chunk).wait_recv()
+        above = totr_v[l, ts].astype(F32)
+        carry_v[ts] = carry + above + tots_v[l, ts].astype(F32)
+        carry = carry + (1 - half).astype(F32) * above
         for i in reversed(range(CHIPS)):
             rs_v[l, i, ts] = carry.astype(BF16)
             carry = carry + q8_v[l, i, ts].astype(F32)
-        carry_v[ts] = carry
-        for j in (4, 2, 6, 1, 3, 5, 7):
+        for j in (2, 1, 3):
             from_owner(chunk, j, chip).start()
         rr_v[l, ts, chip] = rs_v[l, chip, ts]
 
@@ -403,61 +426,84 @@
         out_here(chunk).start()
 
     attention(2)
-    pl.semaphore_wait(barrier, TP + CHIPS - 1)
-    gather_1((2, 0, 2))
+    pl.semaphore_wait(barrier, TP + CHIPS)
+    gather_1((2, 1, 1))
+    gather_1((2, 0, 1))
     attention(1)
     gather_1((1, 0, 2))
-    gather_2((2, 0, 2))
-    gather_3((2, 0, 2))
+    gather_2((2, 1, 1))
     squares_and_low()
     squares_send()
+    gather_3((2, 0, 1))
+    gather_2((2, 0, 1))
+    attention(0)
     gather_2((1, 0, 2))
-    gather_4((2, 0, 2))
-    attention(0)
+    gather_4((2, 0, 1))
+    squares_wait()
+    gather_3((2, 1, 1))
+    gather_4((2, 1, 1))
+    gather_3((1, 0, 2))
     gather_4((1, 0, 2))
-    gather_3((1, 0, 2))
     gather_1((0, 0, 2))
-    gather_end((2, 0, 2))
-    products((2, 0, 2))
+    gather_end((2, 0, 1))
+    products((2, 0, 1))
+    gather_end((2, 1, 1))
+    products((2, 1, 1))
+    gather_end((1, 0, 2))
     gather_2((0, 0, 2))
-    gather_end((1, 0, 2))
     products((1, 0, 2))
-    squares_wait()
-    terms((2, 0, 2))
-    core_copy((2, 0, 2)).start()
+    gather_3((0, 0, 2))
+    terms((2, 0, 1))
+    core_copy((2, 0, 1)).start()
+    terms((2, 1, 1))
+    pair_sums((2, 0, 1))
     gather_4((0, 0, 2))
-    gather_3((0, 0, 2))
-    adapters(1)
-    pair_sums((2, 0, 2))
+    core_copy((2, 1, 1)).start()
+    pair_sums((2, 1, 1))
     terms((1, 0, 2))
     core_copy((1, 0, 2)).start()
+    adapters(2)
+    pair_sums((1, 0, 2))
     gather_end((0, 0, 2))
-    pair_sums((1, 0, 2))
+    totals((2, 0, 1))
     products((0, 0, 2))
-    suffix((2, 0, 2))
+    totals((2, 1, 1))
+    suffix((2, 0, 1))
+    adapters(0)
+    suffix((2, 1, 1))
     terms((0, 0, 2))
-    adapters(2)
-    core_copy((0, 0, 2)).start()
-    pair_sums((0, 0, 2))
+    core_copy((0, 0, 1)).start()
+    totals((1, 0, 2))
+    adapters(1)
+    adapters_end(2)
+    pair_sums((0, 0, 1))
+    core_copy((0, 1, 1)).start()
+    pair_sums((0, 1, 1))
     suffix((1, 0, 2))
-    suffix((0, 0, 2))
-    adapters_end(2)
+    totals((0, 0, 1))
+    finish((2, 0, 1))
+    totals((0, 1, 1))
+    suffix((0, 0, 1))
+    suffix((0, 1, 1))
+    finish((0, 0, 1))
+    adapters_end(0)
+    adapters_end(1)
+    finish((2, 1, 1))
     finish((1, 0, 2))
-    adapters(0)
-    adapters_end(1)
-    finish((2, 0, 2))
-    finish((0, 0, 2))
-    adapters_end(0)
-
-    for chunk in CHUNKS:
+    finish((0, 1, 1))
+
+    for chunk in GATHER_CHUNKS:
+        for i in range(7):
+            gather_out(chunk, i).wait_send()
+    for chunk in PRODUCT_CHUNKS:
+        for j in range(1, TP):
+            inner_copy(chunk, j, tp).wait_send()
+    for chunk in SUM_CHUNKS:
         out_in(chunk).wait_recv()
         out_copy(chunk).wait_send()
         out_here(chunk).wait()
         core_copy(chunk).wait_send()
-        for i in range(7):
-            gather_out(chunk, i).wait_send()
-        for j in range(1, TP):
-            inner_copy(chunk, j, tp).wait_send()
+        total_copy(chunk).wait_send()
         for j in range(1, CHIPS):
             to_owner(chunk, j, chip).wait_send()
             from_owner(chunk, j, chip).wait_send()
@@ -526,6 +572,8 @@
         pltpu.VMEM((LAYERS, CHIPS, 2, ROWS, WIDTH), BF16),
         pltpu.VMEM((LAYERS, 2, CHIPS, ROWS, WIDTH), BF16),
         pltpu.VMEM((2, ROWS, WIDTH), F32),
+        pltpu.VMEM((LAYERS, 2, ROWS, WIDTH), BF16),
+        pltpu.VMEM((LAYERS, 2, ROWS, WIDTH), BF16),
         pltpu.VMEM((LAYERS, 2, HALF, WIDTH), BF16),
         pltpu.VMEM((LAYERS, 2, HALF, WIDTH), BF16),
         dma((16,)), dma((4 * LAYERS,)),
@@ -533,6 +581,7 @@
         dma((LAYERS, 7)), dma((LAYERS, 7)),
         dma((2 * LAYERS,)), dma((2 * LAYERS,)),
         dma((2 * LAYERS, 7)), dma((2 * LAYERS, 7)), dma((2 * LAYERS, 7)), dma((2 * LAYERS, 7)),
+        dma((2 * LAYERS,)), dma((2 * LAYERS,)),
         dma((2 * LAYERS,)), dma((2 * LAYERS,)),
     ]
     grad_in, lora_a, lora_b = pl.pallas_call(

time: 86.9 us -> 81.9 us (0.942)
  Pallas kernels: 85.9 us -> 81 us
    pallas_call x1, Pallas kernels: 82.7 us -> 77.8 us  [per_device(): pl.pallas_call(kernel, name='value_backward', out_shape=(jax.ShapeDtypeSt...]
where the time goes in v3:
time: 81.9 us; the launch traced here: 81.8 us
  Pallas kernels  81 us (99%)
    pallas_call x1, Pallas kernels, per_device(): pl.pallas_call(kernel, name='value_backward', out_shape=(jax.ShapeDtypeSt...  77.8 us
    pallas_call x1, Pallas kernels, per_device(): pl.pallas_call(place, name='place', out_shape=(jax.ShapeDtypeStruct(grad_...  3.22 us

profile of v3, /device:TPU:1, one launch (start us, length us, event | category | flops | bytes accessed | tf_op | source)
XLA Modules:
  0.0 81.8 jit_solution(17086891241328458465)
XLA Ops:
  0.6 77.8 %value_backward.1 = (bf16[3,2,2,128,1024]{4,3,2,1,0:T(8,128)(2,1)}, f32[3,64,1024]{2,1,0:T(8,128)}, f32[3,64,128]{2,1,0:T(8,128)}) custom-call(bf16[3,512,1024]{2,1,0:T(8,128)(2,1)} %bitcast.19, bf16[3,512,1024]{2,1,0:T(8,128)(2,1)} %bitcast.20, bf16[3,512,128]{2,1,0:T(8,128)(2,1)} %bitcast.25, bf16[3,512,1024]{2,1,0:T(8,128)(2,1)} %bitcast.21, ...), custom_call_target="tpu_custom_call" | custom-call | flops 8000000000 | bytes 22000000 | tf_op jit(solution)/shard_map/value_backward/pallas_call | solution.py:587
  78.4 3.2 %place.1 = (bf16[3,2,2,128,1024]{4,3,2,1,0:T(8,128)(2,1)}, f32[3,64,1024]{2,1,0:T(8,128)}, f32[3,64,128]{2,1,0:T(8,128)}) custom-call(bf16[3,2,2,128,1024]{4,3,2,1,0:T(8,128)(2,1)} %get-tuple-element.9.grad_ref, f32[3,64,1024]{2,1,0:T(8,128)} %get-tuple-element.10.a_ref, f32[3,64,128]{2,1,0:T(8,128)} %get-tuple-element.11.b_ref), custom_call_target="tpu_custom_call" | custom-call | tf_op jit(solution)/shard_map/place/pallas_call | solution.py:607

commit v4 on v3

--- a/solution.py
+++ b/solution.py
@@ -22,9 +22,9 @@
 MODEL = 8192
 SEGS = 8
 LOG2E = 1.4426950408889634
-GATHER_CHUNKS = ((2, 1, 1), (2, 0, 1), (1, 0, 2), (0, 0, 2))
-PRODUCT_CHUNKS = ((2, 0, 1), (2, 1, 1), (1, 0, 2), (0, 0, 2))
-SUM_CHUNKS = ((2, 0, 1), (0, 0, 1), (2, 1, 1), (1, 0, 2), (0, 1, 1))
+GATHER_CHUNKS = ((2, 0, 1), (2, 1, 1), (1, 1, 1), (1, 0, 1), (0, 0, 1), (0, 1, 1))
+PRODUCT_CHUNKS = ((2, 0, 1), (2, 1, 1), (1, 0, 1), (1, 1, 1), (0, 0, 1), (0, 1, 1))
+SUM_CHUNKS = ((2, 0, 1), (2, 1, 1), (1, 1, 1), (1, 0, 1), (0, 0, 1), (0, 1, 1))
 SOFTMAX_SCALE = HEAD**-0.5 * LOG2E
 MASK_OFFSET = (0, 128, 384, 768)
 
@@ -427,69 +427,88 @@
 
     attention(2)
     pl.semaphore_wait(barrier, TP + CHIPS)
+    gather_1((2, 0, 1))
     gather_1((2, 1, 1))
-    gather_1((2, 0, 1))
     attention(1)
-    gather_1((1, 0, 2))
-    gather_2((2, 1, 1))
+    gather_1((1, 1, 1))
+    gather_2((2, 0, 1))
+    gather_1((1, 0, 1))
     squares_and_low()
     squares_send()
+    gather_2((2, 1, 1))
+    gather_2((1, 0, 1))
     gather_3((2, 0, 1))
-    gather_2((2, 0, 1))
+    gather_4((2, 0, 1))
+    gather_3((2, 1, 1))
     attention(0)
-    gather_2((1, 0, 2))
-    gather_4((2, 0, 1))
+    gather_2((1, 1, 1))
     squares_wait()
-    gather_3((2, 1, 1))
     gather_4((2, 1, 1))
-    gather_3((1, 0, 2))
-    gather_4((1, 0, 2))
-    gather_1((0, 0, 2))
+    gather_4((1, 0, 1))
+    gather_3((1, 0, 1))
     gather_end((2, 0, 1))
     products((2, 0, 1))
+    gather_4((1, 1, 1))
+    gather_3((1, 1, 1))
+    gather_1((0, 0, 1))
     gather_end((2, 1, 1))
     products((2, 1, 1))
-    gather_end((1, 0, 2))
-    gather_2((0, 0, 2))
-    products((1, 0, 2))
-    gather_3((0, 0, 2))
+    gather_1((0, 1, 1))
+    gather_end((1, 0, 1))
+    products((1, 0, 1))
     terms((2, 0, 1))
     core_copy((2, 0, 1)).start()
+    gather_2((0, 0, 1))
+    gather_end((1, 1, 1))
+    products((1, 1, 1))
+    pair_sums((2, 0, 1))
     terms((2, 1, 1))
-    pair_sums((2, 0, 1))
-    gather_4((0, 0, 2))
+    gather_3((0, 0, 1))
     core_copy((2, 1, 1)).start()
+    gather_2((0, 1, 1))
+    adapters(1)
+    gather_4((0, 0, 1))
+    terms((1, 0, 1))
     pair_sums((2, 1, 1))
-    terms((1, 0, 2))
-    core_copy((1, 0, 2)).start()
+    core_copy((1, 0, 1)).start()
+    terms((1, 1, 1))
+    gather_3((0, 1, 1))
+    core_copy((1, 1, 1)).start()
+    pair_sums((1, 0, 1))
+    gather_4((0, 1, 1))
+    totals((2, 0, 1))
+    gather_end((0, 0, 1))
+    products((0, 0, 1))
+    pair_sums((1, 1, 1))
+    totals((2, 1, 1))
+    gather_end((0, 1, 1))
+    suffix((2, 0, 1))
+    products((0, 1, 1))
+    suffix((2, 1, 1))
+    terms((0, 0, 1))
+    core_copy((0, 0, 1)).start()
     adapters(2)
-    pair_sums((1, 0, 2))
-    gather_end((0, 0, 2))
-    totals((2, 0, 1))
-    products((0, 0, 2))
-    totals((2, 1, 1))
-    suffix((2, 0, 1))
+    totals((1, 0, 1))
+    pair_sums((0, 0, 1))
     adapters(0)
-    suffix((2, 1, 1))
-    terms((0, 0, 2))
-    core_copy((0, 0, 1)).start()
-    totals((1, 0, 2))
-    adapters(1)
-    adapters_end(2)
-    pair_sums((0, 0, 1))
+    terms((0, 1, 1))
     core_copy((0, 1, 1)).start()
+    totals((1, 1, 1))
+    finish((2, 0, 1))
     pair_sums((0, 1, 1))
-    suffix((1, 0, 2))
+    suffix((1, 0, 1))
+    adapters_end(1)
+    suffix((1, 1, 1))
     totals((0, 0, 1))
-    finish((2, 0, 1))
+    adapters_end(0)
     totals((0, 1, 1))
     suffix((0, 0, 1))
+    adapters_end(2)
+    finish((2, 1, 1))
     suffix((0, 1, 1))
+    finish((1, 1, 1))
+    finish((1, 0, 1))
     finish((0, 0, 1))
-    adapters_end(0)
-    adapters_end(1)
-    finish((2, 1, 1))
-    finish((1, 0, 2))
     finish((0, 1, 1))
 
     for chunk in GATHER_CHUNKS:

time: 81.9 us -> 79.1 us (0.966)
  Pallas kernels: 81 us -> 78.1 us
    pallas_call x1, Pallas kernels: 77.8 us -> 74.9 us  [per_device(): pl.pallas_call(kernel, name='value_backward', out_shape=(jax.ShapeDtypeSt...]
where the time goes in v4:
time: 79.1 us; the launch traced here: 78.9 us
  Pallas kernels  78.1 us (99%)
  between operations  0.8 us (1%)
    pallas_call x1, Pallas kernels, per_device(): pl.pallas_call(kernel, name='value_backward', out_shape=(jax.ShapeDtypeSt...  74.9 us
    pallas_call x1, Pallas kernels, per_device(): pl.pallas_call(place, name='place', out_shape=(jax.ShapeDtypeStruct(grad_...  3.22 us

profile of v4, /device:TPU:1, one launch (start us, length us, event | category | flops | bytes accessed | tf_op | source)
XLA Modules:
  0.0 78.9 jit_solution(14359943485001663644)
XLA Ops:
  0.6 74.9 %value_backward.1 = (bf16[3,2,2,128,1024]{4,3,2,1,0:T(8,128)(2,1)}, f32[3,64,1024]{2,1,0:T(8,128)}, f32[3,64,128]{2,1,0:T(8,128)}) custom-call(bf16[3,512,1024]{2,1,0:T(8,128)(2,1)} %bitcast.19, bf16[3,512,1024]{2,1,0:T(8,128)(2,1)} %bitcast.20, bf16[3,512,128]{2,1,0:T(8,128)(2,1)} %bitcast.25, bf16[3,512,1024]{2,1,0:T(8,128)(2,1)} %bitcast.21, ...), custom_call_target="tpu_custom_call" | custom-call | flops 8000000000 | bytes 22000000 | tf_op jit(solution)/shard_map/value_backward/pallas_call | solution.py:606
  75.5 3.2 %place.1 = (bf16[3,2,2,128,1024]{4,3,2,1,0:T(8,128)(2,1)}, f32[3,64,1024]{2,1,0:T(8,128)}, f32[3,64,128]{2,1,0:T(8,128)}) custom-call(bf16[3,2,2,128,1024]{4,3,2,1,0:T(8,128)(2,1)} %get-tuple-element.9.grad_ref, f32[3,64,1024]{2,1,0:T(8,128)} %get-tuple-element.10.a_ref, f32[3,64,128]{2,1,0:T(8,128)} %get-tuple-element.11.b_ref), custom_call_target="tpu_custom_call" | custom-call | tf_op jit(solution)/shard_map/place/pallas_call | solution.py:626

commit v5 on v4

--- a/solution.py
+++ b/solution.py
@@ -22,9 +22,10 @@
 MODEL = 8192
 SEGS = 8
 LOG2E = 1.4426950408889634
-GATHER_CHUNKS = ((2, 0, 1), (2, 1, 1), (1, 1, 1), (1, 0, 1), (0, 0, 1), (0, 1, 1))
+ALONG_CHUNKS = ((2, 0, 1), (1, 1, 1), (0, 1, 1), )
+GATHER_CHUNKS = ((2, 1, 1), (1, 0, 1), (0, 0, 1))
 PRODUCT_CHUNKS = ((2, 0, 1), (2, 1, 1), (1, 0, 1), (1, 1, 1), (0, 0, 1), (0, 1, 1))
-SUM_CHUNKS = ((2, 0, 1), (2, 1, 1), (1, 1, 1), (1, 0, 1), (0, 0, 1), (0, 1, 1))
+SUM_CHUNKS = ((2, 0, 1), (2, 1, 1), (1, 0, 1), (0, 0, 1), (1, 1, 1), (0, 1, 1))
 SOFTMAX_SCALE = HEAD**-0.5 * LOG2E
 MASK_OFFSET = (0, 128, 384, 768)
 
@@ -217,6 +218,53 @@
         for i in (2, 3, 5, 6):
             gather_in(chunk, i).wait_recv()
 
+    def along_copy(chunk, i, place, device, first=0, count=SPAN):
+        part = vg_v.at[chunk[0], place, pl.ds(chunk[1] * SPAN + first, count)]
+        return remote(part, part, gs_sem.at[index(chunk), i], gr_sem.at[index(chunk), i], device)
+
+    def along_out(chunk, i):
+        return (
+            lambda: along_copy(chunk, 0, slot, yl_peer),
+            lambda: along_copy(chunk, 1, slot, x_up),
+            lambda: along_copy(chunk, 2, slot, x_down),
+            lambda: along_copy(chunk, 3, left + yl, yl_peer),
+            lambda: along_copy(chunk, 4, right + yl, yl_peer),
+            lambda: along_copy(chunk, 5, left + yl, x_up, 0, HALF),
+            lambda: along_copy(chunk, 6, right + yl, x_down, HALF, HALF),
+            lambda: along_copy(chunk, 7, across + yl, yl_peer),
+        )[i]()
+
+    def along_in(chunk, i):
+        return (
+            lambda: along_copy(chunk, 0, other, yl_peer),
+            lambda: along_copy(chunk, 1, left + yl, x_up),
+            lambda: along_copy(chunk, 2, right + yl, x_down),
+            lambda: along_copy(chunk, 3, left + (1 - yl), yl_peer),
+            lambda: along_copy(chunk, 4, right + (1 - yl), yl_peer),
+            lambda: along_copy(chunk, 5, across + yl, x_up, 0, HALF),
+            lambda: along_copy(chunk, 6, across + yl, x_down, HALF, HALF),
+            lambda: along_copy(chunk, 7, across + (1 - yl), yl_peer),
+        )[i]()
+
+    def along_1(chunk):
+        for i in (1, 2, 0):
+            along_out(chunk, i).start()
+
+    def along_2(chunk):
+        along_in(chunk, 1).wait_recv()
+        along_in(chunk, 2).wait_recv()
+        for i in (5, 6, 3, 4):
+            along_out(chunk, i).start()
+
+    def along_3(chunk):
+        along_in(chunk, 5).wait_recv()
+        along_in(chunk, 6).wait_recv()
+        along_out(chunk, 7).start()
+
+    def along_end(chunk):
+        for i in (0, 3, 4, 7):
+            along_in(chunk, i).wait_recv()
+
     def squares_and_low():
         sqs_v[...] = jnp.zeros((16, 128), F32)
         copies["h"].wait()
@@ -427,93 +475,93 @@
 
     attention(2)
     pl.semaphore_wait(barrier, TP + CHIPS)
-    gather_1((2, 0, 1))
+    along_1((2, 0, 1))
     gather_1((2, 1, 1))
     attention(1)
-    gather_1((1, 1, 1))
-    gather_2((2, 0, 1))
     gather_1((1, 0, 1))
+    along_1((1, 1, 1))
     squares_and_low()
     squares_send()
+    along_2((2, 0, 1))
     gather_2((2, 1, 1))
     gather_2((1, 0, 1))
-    gather_3((2, 0, 1))
-    gather_4((2, 0, 1))
+    along_3((2, 0, 1))
+    along_2((1, 1, 1))
+    attention(0)
     gather_3((2, 1, 1))
-    attention(0)
-    gather_2((1, 1, 1))
+    gather_4((2, 1, 1))
     squares_wait()
-    gather_4((2, 1, 1))
     gather_4((1, 0, 1))
+    along_3((1, 1, 1))
     gather_3((1, 0, 1))
-    gather_end((2, 0, 1))
+    along_end((2, 0, 1))
     products((2, 0, 1))
-    gather_4((1, 1, 1))
-    gather_3((1, 1, 1))
     gather_1((0, 0, 1))
+    along_1((0, 1, 1))
     gather_end((2, 1, 1))
     products((2, 1, 1))
-    gather_1((0, 1, 1))
     gather_end((1, 0, 1))
     products((1, 0, 1))
+    gather_2((0, 0, 1))
+    gather_3((0, 0, 1))
+    along_end((1, 1, 1))
     terms((2, 0, 1))
     core_copy((2, 0, 1)).start()
-    gather_2((0, 0, 1))
-    gather_end((1, 1, 1))
     products((1, 1, 1))
     pair_sums((2, 0, 1))
     terms((2, 1, 1))
-    gather_3((0, 0, 1))
     core_copy((2, 1, 1)).start()
-    gather_2((0, 1, 1))
-    adapters(1)
+    along_2((0, 1, 1))
     gather_4((0, 0, 1))
     terms((1, 0, 1))
+    core_copy((1, 0, 1)).start()
     pair_sums((2, 1, 1))
-    core_copy((1, 0, 1)).start()
+    adapters(2)
+    pair_sums((1, 0, 1))
+    along_3((0, 1, 1))
     terms((1, 1, 1))
-    gather_3((0, 1, 1))
     core_copy((1, 1, 1)).start()
-    pair_sums((1, 0, 1))
-    gather_4((0, 1, 1))
+    gather_end((0, 0, 1))
     totals((2, 0, 1))
-    gather_end((0, 0, 1))
     products((0, 0, 1))
     pair_sums((1, 1, 1))
     totals((2, 1, 1))
-    gather_end((0, 1, 1))
+    along_end((0, 1, 1))
+    products((0, 1, 1))
     suffix((2, 0, 1))
-    products((0, 1, 1))
+    terms((0, 0, 1))
+    totals((1, 0, 1))
     suffix((2, 1, 1))
-    terms((0, 0, 1))
     core_copy((0, 0, 1)).start()
-    adapters(2)
-    totals((1, 0, 1))
+    totals((1, 1, 1))
+    terms((0, 1, 1))
     pair_sums((0, 0, 1))
-    adapters(0)
-    terms((0, 1, 1))
     core_copy((0, 1, 1)).start()
-    totals((1, 1, 1))
-    finish((2, 0, 1))
     pair_sums((0, 1, 1))
     suffix((1, 0, 1))
-    adapters_end(1)
+    adapters_end(2)
+    adapters(1)
+    adapters(0)
+    finish((2, 0, 1))
+    totals((0, 0, 1))
     suffix((1, 1, 1))
-    totals((0, 0, 1))
-    adapters_end(0)
+    finish((2, 1, 1))
     totals((0, 1, 1))
     suffix((0, 0, 1))
-    adapters_end(2)
-    finish((2, 1, 1))
     suffix((0, 1, 1))
-    finish((1, 1, 1))
     finish((1, 0, 1))
     finish((0, 0, 1))
+    adapters_end(1)
+    adapters_end(0)
+    finish((1, 1, 1))
     finish((0, 1, 1))
 
     for chunk in GATHER_CHUNKS:
         for i in range(7):
             gather_out(chunk, i).wait_send()
+    for chunk in ALONG_CHUNKS:
+        for i in range(8):
+            along_out(chunk, i).wait_send()
     for chunk in PRODUCT_CHUNKS:
         for j in range(1, TP):
             inner_copy(chunk, j, tp).wait_send()
@@ -596,7 +644,7 @@
         pltpu.VMEM((LAYERS, 2, HALF, WIDTH), BF16),
         pltpu.VMEM((LAYERS, 2, HALF, WIDTH), BF16),
         dma((16,)), dma((4 * LAYERS,)),
-        dma((2 * LAYERS, 7)), dma((2 * LAYERS, 7)), dma((7,)), dma((7,)), dma((2 * LAYERS, 7)), dma((2 * LAYERS, 7)),
+        dma((2 * LAYERS, 8)), dma((2 * LAYERS, 8)), dma((7,)), dma((7,)), dma((2 * LAYERS, 7)), dma((2 * LAYERS, 7)),
         dma((LAYERS, 7)), dma((LAYERS, 7)),
         dma((2 * LAYERS,)), dma((2 * LAYERS,)),
         dma((2 * LAYERS, 7)), dma((2 * LAYERS, 7)), dma((2 * LAYERS, 7)), dma((2 * LAYERS, 7)),

time: 79.1 us -> 78.1 us (0.987)
  Pallas kernels: 78.1 us -> 77.1 us
    pallas_call x1, Pallas kernels: 74.9 us -> 73.9 us  [per_device(): pl.pallas_call(kernel, name='value_backward', out_shape=(jax.ShapeDtypeSt...]
where the time goes in v5:
time: 78.1 us; the launch traced here: 77.9 us
  Pallas kernels  77.1 us (99%)
  between operations  0.8 us (1%)
    pallas_call x1, Pallas kernels, per_device(): pl.pallas_call(kernel, name='value_backward', out_shape=(jax.ShapeDtypeSt...  73.9 us
    pallas_call x1, Pallas kernels, per_device(): pl.pallas_call(place, name='place', out_shape=(jax.ShapeDtypeStruct(grad_...  3.22 us

profile of v5, /device:TPU:1, one launch (start us, length us, event | category | flops | bytes accessed | tf_op | source)
XLA Modules:
  0.0 77.9 jit_solution(980898927407129891)
XLA Ops:
  0.6 73.9 %value_backward.1 = (bf16[3,2,2,128,1024]{4,3,2,1,0:T(8,128)(2,1)}, f32[3,64,1024]{2,1,0:T(8,128)}, f32[3,64,128]{2,1,0:T(8,128)}) custom-call(bf16[3,512,1024]{2,1,0:T(8,128)(2,1)} %bitcast.19, bf16[3,512,1024]{2,1,0:T(8,128)(2,1)} %bitcast.20, bf16[3,512,128]{2,1,0:T(8,128)(2,1)} %bitcast.25, bf16[3,512,1024]{2,1,0:T(8,128)(2,1)} %bitcast.21, ...), custom_call_target="tpu_custom_call" | custom-call | flops 8000000000 | bytes 22000000 | tf_op jit(solution)/shard_map/value_backward/pallas_call | solution.py:654
  74.5 3.2 %place.1 = (bf16[3,2,2,128,1024]{4,3,2,1,0:T(8,128)(2,1)}, f32[3,64,1024]{2,1,0:T(8,128)}, f32[3,64,128]{2,1,0:T(8,128)}) custom-call(bf16[3,2,2,128,1024]{4,3,2,1,0:T(8,128)(2,1)} %get-tuple-element.9.grad_ref, f32[3,64,1024]{2,1,0:T(8,128)} %get-tuple-element.10.a_ref, f32[3,64,128]{2,1,0:T(8,128)} %get-tuple-element.11.b_ref), custom_call_target="tpu_custom_call" | custom-call | tf_op jit(solution)/shard_map/place/pallas_call | solution.py:674

commit v6 on v5

--- a/solution.py
+++ b/solution.py
@@ -312,15 +312,15 @@
         acc_v[rows] = jnp.zeros((chunk[2] * SPAN, 128), F32)
 
         def one(n, unused):
-            cols = pl.ds(pl.multiple_of(n * 256, 256), 256)
+            cols = pl.ds(pl.multiple_of(n * 512, 512), 512)
             twice = (ad_v[l, rows].astype(F32) * 2.0).astype(BF16)
             ng = dot(gathered(l, rows), w_v[l, cols, :], ((1,), (1,))) + dot(twice, dn_v[l, :, cols], ((1,), (0,)))
             ng_v[l % 2, rows, cols] = ng
             prod = h_v[l, rows, cols].astype(F32) * ng
-            acc_v[rows] += prod[:, :128] + prod[:, 128:]
+            acc_v[rows] += (prod[:, :128] + prod[:, 128:256]) + (prod[:, 256:384] + prod[:, 384:])
             return unused
 
-        lax.fori_loop(0, WIDTH // 256, one, 0)
+        lax.fori_loop(0, WIDTH // 512, one, 0)
         row = rows_of(acc_v[rows])
         ins_v[at] = jnp.concatenate([row] * (4 // chunk[2]), axis=0)
         inr_v[at, tp] = ins_v[at]

time: 78.1 us -> 77.6 us (level)
  no operation moved by 1% of the time
where the time goes in v6:
time: 77.6 us; the launch traced here: 77.5 us
  Pallas kernels  76.7 us (99%)
  between operations  0.8 us (1%)
    pallas_call x1, Pallas kernels, per_device(): pl.pallas_call(kernel, name='value_backward', out_shape=(jax.ShapeDtypeSt...  73.4 us
    pallas_call x1, Pallas kernels, per_device(): pl.pallas_call(place, name='place', out_shape=(jax.ShapeDtypeStruct(grad_...  3.22 us

profile of v6, /device:TPU:1, one launch (start us, length us, event | category | flops | bytes accessed | tf_op | source)
XLA Modules:
  0.0 77.5 jit_solution(12793099050445814353)
XLA Ops:
  0.6 73.4 %value_backward.1 = (bf16[3,2,2,128,1024]{4,3,2,1,0:T(8,128)(2,1)}, f32[3,64,1024]{2,1,0:T(8,128)}, f32[3,64,128]{2,1,0:T(8,128)}) custom-call(bf16[3,512,1024]{2,1,0:T(8,128)(2,1)} %bitcast.19, bf16[3,512,1024]{2,1,0:T(8,128)(2,1)} %bitcast.20, bf16[3,512,128]{2,1,0:T(8,128)(2,1)} %bitcast.25, bf16[3,512,1024]{2,1,0:T(8,128)(2,1)} %bitcast.21, ...), custom_call_target="tpu_custom_call" | custom-call | flops 8000000000 | bytes 22000000 | tf_op jit(solution)/shard_map/value_backward/pallas_call | solution.py:654
  74.1 3.2 %place.1 = (bf16[3,2,2,128,1024]{4,3,2,1,0:T(8,128)(2,1)}, f32[3,64,1024]{2,1,0:T(8,128)}, f32[3,64,128]{2,1,0:T(8,128)}) custom-call(bf16[3,2,2,128,1024]{4,3,2,1,0:T(8,128)(2,1)} %get-tuple-element.9.grad_ref, f32[3,64,1024]{2,1,0:T(8,128)} %get-tuple-element.10.a_ref, f32[3,64,128]{2,1,0:T(8,128)} %get-tuple-element.11.b_ref), custom_call_target="tpu_custom_call" | custom-call | tf_op jit(solution)/shard_map/place/pallas_call | solution.py:674
